TPU v7x, 32 devices: a whole 2x2x4 slice. The times are simulated.
32 devices in a mesh: seq: 8 (over z, core), head: 4 (over y, x).
Axes of the slice: x: 2, y: 2, z: 4, core: 2. Of those that a mesh axis runs over, the one named last changes fastest.
Arguments:
- queries: bfloat16 [6144, 2048], P('seq', 'head'), may hold values from -8 to 8
- enc_keys: bfloat16 [16384, 2048], P('seq', 'head'), may hold values from -8 to 8
- enc_values: bfloat16 [16384, 2048], P('seq', 'head'), may hold values from -6 to 6
- out_proj: bfloat16 [2048, 2048], P('head'), may hold values from -0.125 to 0.125
- out_grad: bfloat16 [6144, 2048], P(('seq', 'head')), may hold values from -6 to 6
- block_doc: int32 [128], replicated, may hold values from 0 to 63, as said below
- query_doc: int32 [6144], replicated, may hold values from 0 to 63, as said below
Outputs:
- mixed: bfloat16 [6144, 2048], P(('seq', 'head'))
- grad_q: bfloat16 [6144, 2048], P('seq', 'head')
- grad_k: bfloat16 [16384, 2048], P('seq', 'head')
- grad_v: bfloat16 [16384, 2048], P('seq', 'head')
- grad_wo: float32 [2048, 2048], P('head', 'seq')
Inputs may be any that keep to these rules, and one draw needn't show every extreme that they name: `block_doc`: never falls; each document's blocks are consecutive, lie on one sequence shard and number 1 to 3; each shard holds the blocks of exactly 8 documents. `query_doc`: every row belongs to a document; each document has 1 to 144 rows, all consecutive and on one sequence shard of 768 rows; each shard holds the rows of exactly 8 documents, and no two documents whose blocks lie on one shard have their rows on one shard.
All inputs are finite; a program needn't handle non-finite values.
Results may differ from a plain program's by a relative error of at most 0.023.
Values may be sent and summed in bfloat16 or wider, within the bound.
A program may use at most 64 MiB of HBM per device.

v0:
```python
import jax
import jax.numpy as jnp
from jax import lax
from jax.sharding import PartitionSpec as P

HD = 64
BLOCK = 128
BLK = 16
DPS = 8
QMOST = 144


score_scale = 0.125
masked_score = -1e30


def lookup(table, index):
    positions = jnp.arange(table.shape[0], dtype=jnp.int32)
    return jnp.sum(jnp.where(index[:, None] == positions[None, :], table[None, :], 0), axis=1)


def first_true(flags, wanted_count):
    order = jnp.cumsum(flags.astype(jnp.int32)) - 1
    wanted = jnp.arange(wanted_count, dtype=jnp.int32)
    matches = flags[None, :] & (order[None, :] == wanted[:, None])
    positions = jnp.arange(flags.shape[0], dtype=jnp.int32)
    return jnp.sum(jnp.where(matches, positions[None, :], 0), axis=1)


def rank_within(targets, shard_count):
    onehot = (targets[:, None] == jnp.arange(shard_count, dtype=jnp.int32)[None, :]).astype(
        jnp.int32
    )
    before = jnp.cumsum(onehot, axis=0) - onehot
    return jnp.sum(before * onehot, axis=1)


def attend(query_rows, grad_rows, query_docs, key_rows, value_rows, key_docs):
    row_count = query_rows.shape[0]
    heads_here = query_rows.shape[1] // HD
    key_total = key_rows.shape[0]
    key_width = min(256, key_total)
    blocks = key_total // key_width
    query_heads = query_rows.reshape(row_count, heads_here, HD)
    grad_heads = grad_rows.reshape(row_count, heads_here, HD)
    key_heads = key_rows.reshape(blocks, key_width, heads_here, HD)
    value_heads = value_rows.reshape(blocks, key_width, heads_here, HD)
    block_docs = key_docs.reshape(blocks, key_width)

    def scores_of(key_block, doc_block):
        raw_scores = (
            jnp.einsum("rhd,khd->rhk", query_heads, key_block, preferred_element_type=jnp.float32)
            * score_scale
        )
        admitted = (query_docs[:, None] == doc_block[None, :])[:, None, :]
        return (jnp.where(admitted, raw_scores, masked_score), admitted)

    def stats_step(carry, block_item):
        running_max, running_sum = carry
        key_block, doc_block = block_item
        scores, admitted = scores_of(key_block, doc_block)
        new_max = jnp.maximum(running_max, jnp.max(scores, axis=2))
        terms = jnp.where(admitted, jnp.exp(scores - new_max[:, :, None]), 0.0)
        running_sum = running_sum * jnp.exp(running_max - new_max) + jnp.sum(terms, axis=2)
        return ((new_max, running_sum), None)

    start_state = (
        jnp.full((row_count, heads_here), masked_score, jnp.float32),
        jnp.zeros((row_count, heads_here), jnp.float32),
    )
    (running_max, running_sum), _ = lax.scan(stats_step, start_state, (key_heads, block_docs))
    running_sum = jnp.where(running_sum > 0.0, running_sum, 1.0)
    logsum = running_max + jnp.log(running_sum)

    def probs_of(key_block, doc_block):
        scores, admitted = scores_of(key_block, doc_block)
        return jnp.where(admitted, jnp.exp(scores - logsum[:, :, None]), 0.0)

    def output_step(accumulated, block_item):
        key_block, value_block, doc_block = block_item
        weights = probs_of(key_block, doc_block).astype(jnp.bfloat16)
        return (
            accumulated
            + jnp.einsum("rhk,khd->rhd", weights, value_block, preferred_element_type=jnp.float32),
            None,
        )

    accumulated, _ = lax.scan(
        output_step,
        jnp.zeros((row_count, heads_here, HD), jnp.float32),
        (key_heads, value_heads, block_docs),
    )
    attended = accumulated.astype(jnp.bfloat16)
    row_delta = jnp.sum(grad_heads.astype(jnp.float32) * attended.astype(jnp.float32), axis=2)

    def grad_step(accumulated, block_item):
        key_block, value_block, doc_block = block_item
        probabilities = probs_of(key_block, doc_block)
        weights = probabilities.astype(jnp.bfloat16)
        dprobs = jnp.einsum(
            "rhd,khd->rhk", grad_heads, value_block, preferred_element_type=jnp.float32
        )
        dscores = (probabilities * (dprobs - row_delta[:, :, None])).astype(jnp.bfloat16)
        accumulated = accumulated + jnp.einsum(
            "rhk,khd->rhd", dscores, key_block, preferred_element_type=jnp.float32
        )
        key_grads = (
            jnp.einsum("rhk,rhd->khd", dscores, query_heads, preferred_element_type=jnp.float32)
            * score_scale
        ).astype(jnp.bfloat16)
        value_grads = jnp.einsum(
            "rhk,rhd->khd", weights, grad_heads, preferred_element_type=jnp.float32
        ).astype(jnp.bfloat16)
        return (accumulated, (key_grads, value_grads))

    accumulated, (key_grads, value_grads) = lax.scan(
        grad_step,
        jnp.zeros((row_count, heads_here, HD), jnp.float32),
        (key_heads, value_heads, block_docs),
    )
    query_grads = (accumulated * score_scale).astype(jnp.bfloat16)
    return (
        attended.reshape(row_count, -1),
        query_grads.reshape(row_count, -1),
        key_grads.reshape(key_total, -1),
        value_grads.reshape(key_total, -1),
    )


def shards(queries, enc_keys, enc_values, out_proj, out_grad, block_doc, query_doc):
    shard_count = lax.axis_size("seq")
    my_shard = lax.axis_index("seq")
    inner_here = queries.shape[1]
    query_total = queries.shape[0]
    key_total = enc_keys.shape[0]
    local_blocks = key_total // BLOCK
    doc_count = block_doc.shape[0] // BLK * DPS
    full_grad = lax.all_gather(out_grad, "head", axis=0, tiled=True)
    attn_grad = lax.dot_general(
        full_grad, out_proj, (((1,), (1,)), ((), ())), preferred_element_type=jnp.float32
    ).astype(jnp.bfloat16)
    doc_ids = jnp.arange(doc_count, dtype=jnp.int32)
    row_ids = jnp.arange(query_doc.shape[0], dtype=jnp.int32)
    doc_shard = jnp.max(
        jnp.where(query_doc[None, :] == doc_ids[:, None], row_ids[None, :] // query_total, -1),
        axis=1,
    )
    local_query_doc = lax.dynamic_slice_in_dim(query_doc, my_shard * query_total, query_total)
    block_ids = jnp.arange(block_doc.shape[0], dtype=jnp.int32)
    member = block_doc[None, :] == doc_ids[:, None]
    key_shard = jnp.max(jnp.where(member, block_ids[None, :] // local_blocks, -1), axis=1)
    my_docs = lax.dynamic_slice_in_dim(block_doc, my_shard * local_blocks, local_blocks)
    row_dest = lookup(key_shard, local_query_doc)
    send_slot = row_dest * QMOST + rank_within(row_dest, shard_count)
    slot_total = shard_count * QMOST
    send_queries = jnp.zeros((slot_total, inner_here), jnp.bfloat16).at[send_slot].set(queries)
    send_grads = jnp.zeros((slot_total, inner_here), jnp.bfloat16).at[send_slot].set(attn_grad)
    got_queries, got_grads = (
        lax.all_to_all(send_queries, "seq", split_axis=0, concat_axis=0, tiled=True),
        lax.all_to_all(send_grads, "seq", split_axis=0, concat_axis=0, tiled=True),
    )
    owned_docs = first_true(key_shard == my_shard, DPS)
    source_rows = (
        lookup(doc_shard, owned_docs)[:, None] * QMOST + jnp.arange(QMOST, dtype=jnp.int32)[None, :]
    ).reshape(-1)
    row_docs = jnp.repeat(owned_docs, QMOST)
    key_docs = jnp.repeat(my_docs, BLOCK)
    far_attended, far_grads, grad_k, grad_v = attend(
        got_queries[source_rows], got_grads[source_rows], row_docs, enc_keys, enc_values, key_docs
    )
    back_attended = (
        jnp.zeros((slot_total, inner_here), jnp.bfloat16).at[source_rows].set(far_attended)
    )
    back_grads = jnp.zeros((slot_total, inner_here), jnp.bfloat16).at[source_rows].set(far_grads)
    returned_attended, returned_grads = (
        lax.all_to_all(back_attended, "seq", split_axis=0, concat_axis=0, tiled=True),
        lax.all_to_all(back_grads, "seq", split_axis=0, concat_axis=0, tiled=True),
    )
    attended = returned_attended[send_slot]
    grad_q = returned_grads[send_slot]
    mixed_out = lax.psum_scatter(
        jnp.dot(attended, out_proj, preferred_element_type=jnp.float32).astype(jnp.bfloat16),
        "head",
        scatter_dimension=0,
        tiled=True,
    )
    weight_part = lax.dot_general(
        attended, full_grad, (((0,), (0,)), ((), ())), preferred_element_type=jnp.float32
    )
    grad_wo = lax.psum_scatter(
        weight_part.astype(jnp.bfloat16), "seq", scatter_dimension=1, tiled=True
    ).astype(jnp.float32)
    return (mixed_out, grad_q, grad_k, grad_v, grad_wo)


def solution(mesh):
    placed = (
        P("seq", "head"),
        P("seq", "head"),
        P("seq", "head"),
        P("head", None),
        P(("seq", "head"), None),
        P(),
        P(),
    )
    return jax.shard_map(
        shards,
        mesh=mesh,
        in_specs=placed,
        out_specs=(
            P(("seq", "head"), None),
            P("seq", "head"),
            P("seq", "head"),
            P("seq", "head"),
            P("head", "seq"),
        ),
        check_vma=False,
    )
```

profile of v0, /device:TPU:0, one launch (start us, length us, event | category | flops | bytes accessed | tf_op | source)
XLA Modules:
  0.0 432.4 jit_solution(4854652109091930544)
XLA Ops:
  11.3 7.1 %scatter_custom_fusion = bf16[1152,512]{1,0:T(8,128)(2,1)} fusion(s32[768]{0:T(1024)S(1)} %fusion.75, bf16[768,512]{1,0:T(8,128)(2,1)} %param.13, bf16[]{:T(256)} %constant.101.clone.1), kind=kCustom, calls=%fused_computation.82 | custom fusion | bytes 1180160 | tf_op jit(solution)/shard_map/scatter | solution.py:156
  18.5 6.3 %all-to-all-start = ((bf16[8,144,512]{2,1,0:T(8,128)(2,1)}), bf16[8,144,512]{2,1,0:T(8,128)(2,1)S(1)}, u32[]{:S(2)}, u32[]{:S(2)}) async-start(bf16[8,144,512]{2,1,0:T(8,128)(2,1)} %bitcast.183), calls=%async_computation | async-start | bytes 2359296 | tf_op jit(solution)/shard_map/all_to_all | solution.py:159
  27.0 6.2 %reshape.388 = bf16[8,256,8,64]{3,2,1,0:T(8,128)(2,1)} reshape(bf16[2048,512]{1,0:T(8,128)(2,1)} %param.14) | data formatting | bytes 4194304 | tf_op jit(solution)/shard_map/reshape | solution.py:46
  33.1 5.2 %copy.62 = bf16[8,256,8,64]{1,3,2,0:T(8,128)(2,1)} copy(bf16[8,256,8,64]{3,2,1,0:T(8,128)(2,1)} %reshape.388) | data formatting | bytes 4194304
  38.4 6.2 %reshape.387 = bf16[8,256,8,64]{3,2,1,0:T(8,128)(2,1)} reshape(bf16[2048,512]{1,0:T(8,128)(2,1)} %param.15) | data formatting | bytes 4194304 | tf_op jit(solution)/shard_map/reshape | solution.py:47
  44.5 5.1 %copy.61 = bf16[8,256,8,64]{1,3,2,0:T(8,128)(2,1)} copy(bf16[8,256,8,64]{3,2,1,0:T(8,128)(2,1)} %reshape.387) | data formatting | bytes 4194304
  49.7 4.5 %all-to-all-done = bf16[8,144,512]{2,1,0:T(8,128)(2,1)S(1)} async-done(((bf16[8,144,512]{2,1,0:T(8,128)(2,1)}), bf16[8,144,512]{2,1,0:T(8,128)(2,1)S(1)}, u32[]{:S(2)}, u32[]{:S(2)}) %all-to-all-start) | async-done | bytes 1179680 | tf_op jit(solution)/shard_map/all_to_all | solution.py:159
  54.2 4.7 %gather_fusion = bf16[1152,512]{1,0:T(8,128)(2,1)} fusion(bf16[1152,512]{1,0:T(8,128)(2,1)S(1)} %bitcast.178, s32[2048]{0:T(1024)S(1)} %pad_clamp_fusion), kind=kCustom, calls=%fused_computation | custom fusion | bytes 2363904 | tf_op jit(solution)/shard_map/gather | solution.py:169
  60.5 43.4 %while.39 = (s32[]{:T(128)}, f32[1152,8]{0,1:T(8,128)S(1)}, f32[1152,8]{0,1:T(8,128)S(1)}, s32[8,256]{1,0:T(8,128)S(1)}, bf16[8,256,8,64]{1,3,2,0:T(8,128)(2,1)}...) while((s32[]{:T(128)}, f32[1152,8]{0,1:T(8,128)S(1)}, ...), condition=%wide.region_13.14_spmd.clone, body=%wide.region_10.13_spmd.clone.sunk | while | flops 321205248 | bytes 21701784 | solution.py:71
  61.0 2.6 fusion.113
  66.4 2.6 fusion.113
  71.8 2.6 fusion.113
  77.2 2.6 fusion.113
  82.7 2.6 fusion.113
  88.1 2.6 fusion.113
  93.5 2.6 fusion.113
  98.9 2.6 fusion.113
  104.0 5.0 %convolution_convert_fusion.2 = bf16[768,512]{1,0:T(8,128)(2,1)} fusion(bf16[768,2048]{1,0:T(8,128)(2,1)} %all-gather.2.cloned.1.call-done, bf16[512,2048]{1,0:T(8,128)(2,1)S(1)} %copy-done), kind=kOutput, calls=%fused_computation.75 | convolution fusion | flops 1611005952 | bytes 6029312 | tf_op jit(solution)/shard_map/dot_general | solution.py:139
  109.0 7.5 %scatter_custom_fusion.2 = bf16[1152,512]{1,0:T(8,128)(2,1)} fusion(s32[768]{0:T(1024)S(1)} %fusion.75, bf16[768,512]{1,0:T(8,128)(2,1)} %convolution_convert_fusion.2, bf16[]{:T(256)} %constant.101.clone.1), kind=kCustom, calls=%fused_computation.78 | custom fusion | bytes 1180160 | tf_op jit(solution)/shard_map/scatter | solution.py:157
  116.5 3.6 all-to-all-start.2
  120.0 65.6 %while.40 = (s32[]{:T(128)}, f32[1152,8,64]{0,2,1:T(8,128)}, bf16[8,256,8,64]{1,3,2,0:T(8,128)(2,1)}, s32[8,256]{1,0:T(8,128)S(1)}, bf16[8,256,8,64]{1,3,2,0:T(8...) while((s32[]{:T(128)}, f32[1152,8,64]{0,2,1:T(8,128)}, ...), condition=%wide.region_15.16_spmd.clone, body=%wide.region_14.15_spmd.clone.sunk | while | flops 617250816 | bytes 7072410 | solution.py:88
  121.2 6.4 %fusion.118 = f32[1152,8,64]{0,2,1:T(8,128)} fusion(f32[1152,8,64]{0,2,1:T(8,128)} %get-tuple-element.612, bf16[1152,8,64]{0,2,1:T(8,128)(2,1)} %get-tuple-element.626, f32[1152,8]{0,1:T(8,128)S(1)} %get-tuple-element.627, pred[1152,256]{0,1:T(8,128)(4,1)} %broadcast_compare_fusion.9, pred[]{:T(512)S(6)} %compare.16, ...), kind=kOutput, calls=%fused_computation.29.clone.1 | convolution fusion | flops 616955904 | bytes 6755840 | tf_op jit(solution)/shard_map/while/body/eval_jaxpr/rhk,khd->rhd/dot_general | solution.py:84
  128.7 7.2 %fusion.118 = f32[1152,8,64]{0,2,1:T(8,128)} fusion(f32[1152,8,64]{0,2,1:T(8,128)} %get-tuple-element.612, bf16[1152,8,64]{0,2,1:T(8,128)(2,1)} %get-tuple-element.626, f32[1152,8]{0,1:T(8,128)S(1)} %get-tuple-element.627, pred[1152,256]{0,1:T(8,128)(4,1)} %broadcast_compare_fusion.9, pred[]{:T(512)S(6)} %compare.16, ...), kind=kOutput, calls=%fused_computation.29.clone.1 | convolution fusion | flops 616955904 | bytes 6755840 | tf_op jit(solution)/shard_map/while/body/eval_jaxpr/rhk,khd->rhd/dot_general | solution.py:84
  137.0 7.2 %fusion.118 = f32[1152,8,64]{0,2,1:T(8,128)} fusion(f32[1152,8,64]{0,2,1:T(8,128)} %get-tuple-element.612, bf16[1152,8,64]{0,2,1:T(8,128)(2,1)} %get-tuple-element.626, f32[1152,8]{0,1:T(8,128)S(1)} %get-tuple-element.627, pred[1152,256]{0,1:T(8,128)(4,1)} %broadcast_compare_fusion.9, pred[]{:T(512)S(6)} %compare.16, ...), kind=kOutput, calls=%fused_computation.29.clone.1 | convolution fusion | flops 616955904 | bytes 6755840 | tf_op jit(solution)/shard_map/while/body/eval_jaxpr/rhk,khd->rhd/dot_general | solution.py:84
  145.3 7.2 %fusion.118 = f32[1152,8,64]{0,2,1:T(8,128)} fusion(f32[1152,8,64]{0,2,1:T(8,128)} %get-tuple-element.612, bf16[1152,8,64]{0,2,1:T(8,128)(2,1)} %get-tuple-element.626, f32[1152,8]{0,1:T(8,128)S(1)} %get-tuple-element.627, pred[1152,256]{0,1:T(8,128)(4,1)} %broadcast_compare_fusion.9, pred[]{:T(512)S(6)} %compare.16, ...), kind=kOutput, calls=%fused_computation.29.clone.1 | convolution fusion | flops 616955904 | bytes 6755840 | tf_op jit(solution)/shard_map/while/body/eval_jaxpr/rhk,khd->rhd/dot_general | solution.py:84
  153.6 7.2 %fusion.118 = f32[1152,8,64]{0,2,1:T(8,128)} fusion(f32[1152,8,64]{0,2,1:T(8,128)} %get-tuple-element.612, bf16[1152,8,64]{0,2,1:T(8,128)(2,1)} %get-tuple-element.626, f32[1152,8]{0,1:T(8,128)S(1)} %get-tuple-element.627, pred[1152,256]{0,1:T(8,128)(4,1)} %broadcast_compare_fusion.9, pred[]{:T(512)S(6)} %compare.16, ...), kind=kOutput, calls=%fused_computation.29.clone.1 | convolution fusion | flops 616955904 | bytes 6755840 | tf_op jit(solution)/shard_map/while/body/eval_jaxpr/rhk,khd->rhd/dot_general | solution.py:84
  161.9 7.2 %fusion.118 = f32[1152,8,64]{0,2,1:T(8,128)} fusion(f32[1152,8,64]{0,2,1:T(8,128)} %get-tuple-element.612, bf16[1152,8,64]{0,2,1:T(8,128)(2,1)} %get-tuple-element.626, f32[1152,8]{0,1:T(8,128)S(1)} %get-tuple-element.627, pred[1152,256]{0,1:T(8,128)(4,1)} %broadcast_compare_fusion.9, pred[]{:T(512)S(6)} %compare.16, ...), kind=kOutput, calls=%fused_computation.29.clone.1 | convolution fusion | flops 616955904 | bytes 6755840 | tf_op jit(solution)/shard_map/while/body/eval_jaxpr/rhk,khd->rhd/dot_general | solution.py:84
  170.2 7.2 %fusion.118 = f32[1152,8,64]{0,2,1:T(8,128)} fusion(f32[1152,8,64]{0,2,1:T(8,128)} %get-tuple-element.612, bf16[1152,8,64]{0,2,1:T(8,128)(2,1)} %get-tuple-element.626, f32[1152,8]{0,1:T(8,128)S(1)} %get-tuple-element.627, pred[1152,256]{0,1:T(8,128)(4,1)} %broadcast_compare_fusion.9, pred[]{:T(512)S(6)} %compare.16, ...), kind=kOutput, calls=%fused_computation.29.clone.1 | convolution fusion | flops 616955904 | bytes 6755840 | tf_op jit(solution)/shard_map/while/body/eval_jaxpr/rhk,khd->rhd/dot_general | solution.py:84
  178.5 7.2 %fusion.118 = f32[1152,8,64]{0,2,1:T(8,128)} fusion(f32[1152,8,64]{0,2,1:T(8,128)} %get-tuple-element.612, bf16[1152,8,64]{0,2,1:T(8,128)(2,1)} %get-tuple-element.626, f32[1152,8]{0,1:T(8,128)S(1)} %get-tuple-element.627, pred[1152,256]{0,1:T(8,128)(4,1)} %broadcast_compare_fusion.9, pred[]{:T(512)S(6)} %compare.16, ...), kind=kOutput, calls=%fused_computation.29.clone.1 | convolution fusion | flops 616955904 | bytes 6755840 | tf_op jit(solution)/shard_map/while/body/eval_jaxpr/rhk,khd->rhd/dot_general | solution.py:84
  185.7 4.7 %gather_fusion.2 = bf16[1152,512]{1,0:T(8,128)(2,1)} fusion(bf16[1152,512]{1,0:T(8,128)(2,1)S(1)} %bitcast.179, s32[2048]{0:T(1024)S(1)} %pad_clamp_fusion), kind=kCustom, calls=%fused_computation.2 | custom fusion | bytes 2363904 | tf_op jit(solution)/shard_map/gather | solution.py:169
  192.0 3.0 multiply_reduce_fusion
  195.0 2.4 copy.63
  197.4 9.5 %scatter_custom_fusion.1 = bf16[1152,512]{1,0:T(8,128)(2,1)} fusion(s32[1152]{0:T(1024)S(1)} %fusion.73, bf16[1152,512]{1,0:T(8,128)(2,1)} %copy.63, bf16[]{:T(256)} %constant.101.clone.1), kind=kCustom, calls=%fused_computation.80 | custom fusion | bytes 1180160 | tf_op jit(solution)/shard_map/scatter | solution.py:172
  206.9 5.0 %all-to-all-start.1 = ((bf16[8,144,512]{2,1,0:T(8,128)(2,1)}), bf16[8,144,512]{2,1,0:T(8,128)(2,1)}, u32[]{:S(2)}, u32[]{:S(2)}) async-start(bf16[8,144,512]{2,1,0:T(8,128)(2,1)} %bitcast.185), calls=%async_computation.1 | async-start | bytes 2359296 | tf_op jit(solution)/shard_map/all_to_all | solution.py:176
  211.9 29.5 %all-to-all-done.1 = bf16[8,144,512]{2,1,0:T(8,128)(2,1)} async-done(((bf16[8,144,512]{2,1,0:T(8,128)(2,1)}), bf16[8,144,512]{2,1,0:T(8,128)(2,1)}, u32[]{:S(2)}, u32[]{:S(2)}) %all-to-all-start.1) | async-done | bytes 1179680 | tf_op jit(solution)/shard_map/all_to_all | solution.py:176
  241.4 5.0 %gather_fusion.1 = bf16[768,512]{1,0:T(8,128)(2,1)} fusion(bf16[1152,512]{1,0:T(8,128)(2,1)} %bitcast.11, s32[1024]{0:T(1024)S(1)} %pad_clamp_fusion.1), kind=kCustom, calls=%fused_computation.1 | custom fusion | bytes 1575936 | tf_op jit(solution)/shard_map/gather | solution.py:179
  246.3 5.3 %convolution_convert_fusion.1 = bf16[512,2048]{1,0:T(8,128)(2,1)} fusion(bf16[768,512]{1,0:T(8,128)(2,1)} %gather_fusion.1, bf16[768,2048]{1,0:T(8,128)(2,1)} %all-gather.2.cloned.1.call-done), kind=kOutput, calls=%fused_computation.70 | convolution fusion | flops 1611661312 | bytes 6029312 | tf_op jit(solution)/shard_map/dot_general | solution.py:187
  251.8 4.6 %convolution_convert_fusion = bf16[768,2048]{1,0:T(8,128)(2,1)} fusion(bf16[768,512]{1,0:T(8,128)(2,1)} %gather_fusion.1, bf16[512,2048]{1,0:T(8,128)(2,1)S(1)} %copy-done), kind=kOutput, calls=%fused_computation.69 | convolution fusion | flops 1612185600 | bytes 6029312 | tf_op jit(solution)/shard_map/dot_general | solution.py:182
  257.7 118.1 %while.41 = (s32[]{:T(128)}, f32[1152,8,64]{0,2,1:T(8,128)}, bf16[8,256,8,64]{1,3,2,0:T(8,128)(2,1)}, bf16[8,256,8,64]{1,3,2,0:T(8,128)(2,1)}, bf16[8,256,8,64]{...) while((s32[]{:T(128)}, f32[1152,8,64]{0,2,1:T(8,128)}, ...), condition=%wide.region_21.22_spmd.clone, body=%wide.region_20.21_spmd.clone.sunk | while | flops 1530691584 | bytes 72774920 | solution.py:116
  258.1 3.7 fusion.129
  264.1 2.4 fusion.130
  272.8 3.7 fusion.129
  278.8 2.4 fusion.130
  287.6 3.7 fusion.129
  293.6 2.4 fusion.130
  302.4 3.7 fusion.129
  308.4 2.4 fusion.130
  317.1 3.7 fusion.129
  323.1 2.4 fusion.130
  325.5 2.3 fusion.132
  331.9 3.7 fusion.129
  337.9 2.4 fusion.130
  346.7 3.7 fusion.129
  352.7 2.4 fusion.130
  361.5 3.7 fusion.129
  367.4 2.4 fusion.130
  378.3 9.1 %scatter_custom_fusion.3 = bf16[1152,512]{1,0:T(8,128)(2,1)} fusion(s32[1152]{0:T(1024)S(1)} %fusion.73, bf16[1152,512]{1,0:T(8,128)(2,1)S(1)} %copy.67, bf16[]{:T(256)} %constant.101.clone.1), kind=kCustom, calls=%fused_computation.76 | custom fusion | bytes 1179650 | tf_op jit(solution)/shard_map/scatter | solution.py:174
  387.4 3.8 all-to-all-start.3
  391.2 3.6 copy.77
  394.9 6.6 %reshape.386 = bf16[2048,512]{1,0:T(8,128)(2,1)} reshape(bf16[8,256,8,64]{3,2,1,0:T(8,128)(2,1)} %copy.77) | data formatting | bytes 4194304
  401.5 3.6 copy.76
  405.1 6.4 %reshape.385 = bf16[2048,512]{1,0:T(8,128)(2,1)} reshape(bf16[8,256,8,64]{3,2,1,0:T(8,128)(2,1)} %copy.76) | data formatting | bytes 4194304
  411.5 9.0 %all-to-all-done.3 = bf16[8,144,512]{2,1,0:T(8,128)(2,1)S(1)} async-done(((bf16[8,144,512]{2,1,0:T(8,128)(2,1)}), bf16[8,144,512]{2,1,0:T(8,128)(2,1)S(1)}, u32[]{:S(2)}, u32[]{:S(2)}) %all-to-all-start.3) | async-done | bytes 1179680 | tf_op jit(solution)/shard_map/all_to_all | solution.py:177
  420.5 3.3 gather_fusion.3
  (252 shorter events, 112.5 us)
Async XLA Ops:
  7.2 96.8 %copy-start = (bf16[512,2048]{1,0:T(8,128)(2,1)S(1)}, bf16[512,2048]{1,0:T(8,128)(2,1)}, u32[]{:S(2)}) copy-start(bf16[512,2048]{1,0:T(8,128)(2,1)} %param.16) | copy-start | bytes 6291460
  11.3 14.2 %copy-start.9 = (s32[128]{0:T(128)S(1)}, s32[128]{0:T(128)}, u32[]{:S(2)}) copy-start(s32[128]{0:T(128)} %param.18) | copy-start | bytes 1540
  11.3 14.9 %copy-start.8 = (s32[6144]{0:T(1024)S(1)}, s32[6144]{0:T(1024)}, u32[]{:S(2)}) copy-start(s32[6144]{0:T(1024)} %param.19) | copy-start | bytes 73732
  18.5 35.7 %all-to-all-start = ((bf16[8,144,512]{2,1,0:T(8,128)(2,1)}), bf16[8,144,512]{2,1,0:T(8,128)(2,1)S(1)}, u32[]{:S(2)}, u32[]{:S(2)}) async-start(bf16[8,144,512]{2,1,0:T(8,128)(2,1)} %bitcast.183), calls=%async_computation | async-start | bytes 2359296 | tf_op jit(solution)/shard_map/all_to_all | solution.py:159
  24.8 79.2 %all-gather.2.cloned.1.call-start = ((), (), s32[]{:S(2)}) async-start(), calls=%async_computation.7 | async-start | bytes 3932160 | tf_op jit(solution)/shard_map/all_gather | solution.py:138
  103.9 5.0 %copy-start.4 = (bf16[1152,8,64]{0,2,1:T(8,128)(2,1)}, bf16[1152,8,64]{0,2,1:T(8,128)(2,1)S(1)}, u32[]{:S(2)}) copy-start(bf16[1152,8,64]{0,2,1:T(8,128)(2,1)S(1)} %get-tuple-element.679) | copy-start | bytes 3538948
  116.5 69.2 %all-to-all-start.2 = ((bf16[8,144,512]{2,1,0:T(8,128)(2,1)}), bf16[8,144,512]{2,1,0:T(8,128)(2,1)S(1)}, u32[]{:S(2)}, u32[]{:S(2)}) async-start(bf16[8,144,512]{2,1,0:T(8,128)(2,1)} %bitcast.184), calls=%async_computation.3 | async-start | bytes 2359296 | tf_op jit(solution)/shard_map/all_to_all | solution.py:160
  206.9 34.5 %all-to-all-start.1 = ((bf16[8,144,512]{2,1,0:T(8,128)(2,1)}), bf16[8,144,512]{2,1,0:T(8,128)(2,1)}, u32[]{:S(2)}, u32[]{:S(2)}) async-start(bf16[8,144,512]{2,1,0:T(8,128)(2,1)} %bitcast.185), calls=%async_computation.1 | async-start | bytes 2359296 | tf_op jit(solution)/shard_map/all_to_all | solution.py:176
  211.9 212.0 %reduce-scatter.5.cloned.1.call-start = ((), (), s32[]{:S(2)}) async-start(), calls=%async_computation.8 | async-start | bytes 2359296 | tf_op jit(solution)/shard_map/reduce_scatter | solution.py:190
  251.7 173.9 %reduce-scatter.3.cloned.1.call-start = ((), (), s32[]{:S(2)}) async-start(), calls=%async_computation.6 | async-start | bytes 3932160 | tf_op jit(solution)/shard_map/reduce_scatter | solution.py:181
  256.4 1.3 copy-start.5
  266.5 2.3 copy-start.2
  271.0 1.4 copy-start.3
  281.2 2.3 copy-start.2
  285.8 1.4 copy-start.3
  296.0 2.3 copy-start.2
  300.5 1.4 copy-start.3
  310.7 2.3 copy-start.2
  315.3 1.4 copy-start.3
  325.5 2.3 copy-start.2
  330.1 1.4 copy-start.3
  340.3 2.3 copy-start.2
  344.9 1.4 copy-start.3
  355.1 2.3 copy-start.2
  359.6 1.4 copy-start.3
  369.8 2.3 copy-start.2
  374.4 1.4 copy-start.3
  378.3 12.9 %copy-start.6 = (bf16[8,256,8,64]{1,3,2,0:T(8,128)(2,1)S(1)}, bf16[8,256,8,64]{1,3,2,0:T(8,128)(2,1)}, u32[]{:S(2)}) copy-start(bf16[8,256,8,64]{1,3,2,0:T(8,128)(2,1)} %get-tuple-element.154) | copy-start | bytes 6291460
  387.4 33.1 %all-to-all-start.3 = ((bf16[8,144,512]{2,1,0:T(8,128)(2,1)}), bf16[8,144,512]{2,1,0:T(8,128)(2,1)S(1)}, u32[]{:S(2)}, u32[]{:S(2)}) async-start(bf16[8,144,512]{2,1,0:T(8,128)(2,1)} %bitcast.16), calls=%async_computation.4 | async-start | bytes 2359296 | tf_op jit(solution)/shard_map/all_to_all | solution.py:177
  394.9 6.6 %copy-start.7 = (bf16[8,256,8,64]{1,3,2,0:T(8,128)(2,1)S(1)}, bf16[8,256,8,64]{1,3,2,0:T(8,128)(2,1)}, u32[]{:S(2)}) copy-start(bf16[8,256,8,64]{1,3,2,0:T(8,128)(2,1)} %get-tuple-element.153) | copy-start | bytes 6291460
  420.5 5.1 %copy-start.1 = (bf16[512,2048]{1,0:T(8,128)(2,1)S(1)}, bf16[512,2048]{1,0:T(8,128)(2,1)}, u32[]{:S(2)}) copy-start(bf16[512,2048]{1,0:T(8,128)(2,1)} %param.16) | copy-start | bytes 6291460
Sparse Core Ops, SparseCore 0:
  27.5 45.4 all-gather.1
  251.8 34.6 reduce-scatter.4
  290.1 42.8 reduce-scatter.2
where the time goes:
time: 438 us; the launch traced here: 432 us
  matrix products  196 us (45%)
  local copies, waits for them, and re-layouts  118 us (27%)
  waiting for transfers between devices  43.4 us (10%)
  other arithmetic  40.4 us (9%)
  starting transfers between devices  19 us (4%)
  between operations  14.3 us (3%)
    dot_general x8, matrix products, output_step(): jnp.einsum('rhk,khd->rhd', weights, value_block, preferred_element_type=j...  56.7 us
    dot_general x16, matrix products, scores_of(): jnp.einsum('rhd,khd->rhk', query_heads, key_block, preferred_element_type...  50.8 us
    unnamed x22, local copies, waits for them, and re-layouts  31.9 us
    all_to_all x1, waiting for transfers between devices, shards(): lax.all_to_all(back_attended, 'seq', split_axis=0, concat_axis=0, tiled=T...  29.5 us
    dot_general x8, matrix products, grad_step(): jnp.einsum('rhd,khd->rhk', grad_heads, value_block, preferred_element_typ...  19 us
    scatter x2, local copies, waits for them, and re-layouts, shards(): jnp.zeros((slot_total, inner_here), jnp.bfloat16).at[source_rows]  18.6 us
    reduce_sum x8, other arithmetic, stats_step(): jnp.sum(terms, axis=2)  18.2 us
    dot_general x8, matrix products, grad_step(): jnp.einsum('rhk,khd->rhd', dscores, key_block, preferred_element_type=jnp...  18.2 us
  transfers between devices with their start and end apart: 7, of which 3 were waited for; matrix products, arithmetic and copies ran while one was open for 66% of the time, Pallas kernels for 0%

commit v1 on v0

v1 whole, which is shorter than its diff:
```python
import functools

import jax
import jax.numpy as jnp
from jax import lax
from jax.experimental import pallas as pl
from jax.experimental.pallas import tpu as pltpu
from jax.sharding import PartitionSpec as P

HD = 64
BLOCK = 128
BLK = 16
DPS = 8
CAP = 3
QMOST = 144
PAIR = 2 * HD
VMEM_LIMIT = 48 * 1024 * 1024

score_scale = 0.125

NT = (((1,), (1,)), ((), ()))
TN = (((0,), (0,)), ((), ()))
NN = (((1,), (0,)), ((), ()))


def mm(a, b, dims):
    return lax.dot_general(a, b, dims, preferred_element_type=jnp.float32)


def scatter_rows(docs, rows, out_ref):
    row_count = rows.shape[0]
    shard_count = out_ref.shape[0] // QMOST
    dest = docs // DPS
    lane = lax.broadcasted_iota(jnp.int32, (1, row_count), 1)
    rank = lax.broadcasted_iota(jnp.int32, (QMOST, row_count), 0)
    for t in range(shard_count):
        mine = dest == t
        start = jnp.min(jnp.where(mine, lane, row_count), axis=1, keepdims=True)
        place = jnp.where(mine, lane - start, -1)
        onehot = jnp.where(rank == place, 1.0, 0.0).astype(jnp.bfloat16)
        out_ref[t * QMOST : (t + 1) * QMOST, :] = mm(onehot, rows, NN).astype(jnp.bfloat16)


def send_kernel(docs_ref, rows_ref, out_ref):
    scatter_rows(docs_ref[...], rows_ref[...], out_ref)


def grad_send_kernel(docs_ref, grad_ref, proj_ref, out_ref):
    attn_grad = mm(grad_ref[...], proj_ref[...], NT).astype(jnp.bfloat16)
    scatter_rows(docs_ref[...], attn_grad, out_ref)


def collect_rows(docs, slots):
    row_count = docs.shape[1]
    slot_total = slots.shape[0]
    dest = docs // DPS
    lane = lax.broadcasted_iota(jnp.int32, (1, row_count), 1)
    slot = jnp.zeros((1, row_count), jnp.int32)
    for t in range(slot_total // QMOST):
        mine = dest == t
        start = jnp.min(jnp.where(mine, lane, row_count), axis=1, keepdims=True)
        slot = jnp.where(mine, t * QMOST + lane - start, slot)
    onehot = jnp.where(
        lax.broadcasted_iota(jnp.int32, (slot_total, row_count), 0) == slot, 1.0, 0.0
    ).astype(jnp.bfloat16)
    return mm(onehot, slots, TN).astype(jnp.bfloat16)


def collect_kernel(docs_ref, slots_ref, out_ref):
    out_ref[...] = collect_rows(docs_ref[...], slots_ref[...])


def project_kernel(docs_ref, slots_ref, proj_ref, grad_ref, mixed_ref, weight_ref):
    attended = collect_rows(docs_ref[...], slots_ref[...])
    mixed_ref[...] = mm(attended, proj_ref[...], NN).astype(jnp.bfloat16)
    weight_ref[...] = mm(attended, grad_ref[...], TN).astype(jnp.bfloat16)


def attend_kernel(first_ref, count_ref, q_ref, g_ref, k_ref, v_ref, att_ref, gq_ref, gk_ref, gv_ref):
    slot = pl.program_id(0)
    count = count_ref[slot]
    inner = q_ref.shape[1]
    low = lax.broadcasted_iota(jnp.int32, (QMOST, PAIR), 1) < HD

    @pl.when(count == 0)
    def _():
        att_ref[...] = jnp.zeros_like(att_ref)
        gq_ref[...] = jnp.zeros_like(gq_ref)

    def work(blocks):
        keys_here = pl.ds(pl.multiple_of(first_ref[slot] * BLOCK, BLOCK), blocks * BLOCK)

        def split(rows):
            zero = jnp.zeros_like(rows)
            return jnp.concatenate([jnp.where(low, rows, zero), jnp.where(low, zero, rows)], axis=0)

        def join(rows):
            return jnp.where(low, rows[:QMOST], rows[QMOST:])

        for c in range(inner // PAIR):
            columns = slice(c * PAIR, (c + 1) * PAIR)
            q2 = split(q_ref[:, columns])
            g2 = split(g_ref[:, columns])
            k = k_ref[keys_here, columns]
            v = v_ref[keys_here, columns]
            scores = mm(q2, k, NT) * score_scale
            terms = jnp.exp(scores - jnp.max(scores, axis=1, keepdims=True))
            probs = terms * (1.0 / jnp.sum(terms, axis=1, keepdims=True))
            weights = probs.astype(jnp.bfloat16)
            attended = mm(weights, v, NN).astype(jnp.bfloat16)
            att_ref[:, columns] = join(attended)
            delta = jnp.sum(
                g2.astype(jnp.float32) * attended.astype(jnp.float32), axis=1, keepdims=True
            )
            dprobs = mm(g2, v, NT)
            dscores = (probs * (dprobs - delta)).astype(jnp.bfloat16)
            gq_ref[:, columns] = join(mm(dscores, k, NN) * score_scale).astype(jnp.bfloat16)
            gk_ref[keys_here, columns] = (mm(dscores, q2, TN) * score_scale).astype(jnp.bfloat16)
            gv_ref[keys_here, columns] = mm(weights, g2, TN).astype(jnp.bfloat16)

    for blocks in range(1, CAP + 1):
        pl.when(count == blocks)(functools.partial(work, blocks))


def call(kernel, outs, flops, *operands):
    whole = pl.BlockSpec(memory_space=pltpu.VMEM)
    moved = sum(x.size * x.dtype.itemsize for x in (*operands, *outs))
    return pl.pallas_call(
        kernel,
        out_shape=outs,
        in_specs=[whole] * len(operands),
        out_specs=[whole] * len(outs),
        compiler_params=pltpu.CompilerParams(vmem_limit_bytes=VMEM_LIMIT),
        cost_estimate=pl.CostEstimate(flops=flops, bytes_accessed=moved, transcendentals=0),
    )(*operands)


def attend(first, count, queries, grads, keys, values):
    slot_total, inner = queries.shape
    rows = pl.BlockSpec((QMOST, inner), lambda s, first, count: (s, 0))
    whole = pl.BlockSpec(keys.shape, lambda s, first, count: (0, 0))
    shapes = [jax.ShapeDtypeStruct(x.shape, jnp.bfloat16) for x in (queries, queries, keys, keys)]
    work = slot_total * keys.shape[0] // DPS * inner
    return pl.pallas_call(
        attend_kernel,
        grid_spec=pltpu.PrefetchScalarGridSpec(
            num_scalar_prefetch=2,
            grid=(slot_total // QMOST,),
            in_specs=[rows, rows, whole, whole],
            out_specs=[rows, rows, whole, whole],
        ),
        out_shape=shapes,
        compiler_params=pltpu.CompilerParams(vmem_limit_bytes=VMEM_LIMIT),
        cost_estimate=pl.CostEstimate(
            flops=40 * work, bytes_accessed=16 * 1024 * 1024, transcendentals=work // HD
        ),
    )(first, count, queries, grads, keys, values)


def shards(queries, enc_keys, enc_values, out_proj, out_grad, block_doc, query_doc):
    shard_count = lax.axis_size("seq")
    my_shard = lax.axis_index("seq")
    query_total, inner_here = queries.shape
    width = out_grad.shape[1]
    local_blocks = enc_keys.shape[0] // BLOCK
    slot_total = shard_count * QMOST

    docs_of = query_doc.reshape(shard_count, query_total)
    local_docs = lax.dynamic_slice_in_dim(docs_of, my_shard, 1)
    my_blocks = lax.dynamic_slice_in_dim(block_doc, my_shard * local_blocks, local_blocks)
    arriving = jnp.max(jnp.where(docs_of // DPS == my_shard, docs_of, -1), axis=1)
    first = jnp.sum((my_blocks[None, :] < arriving[:, None]).astype(jnp.int32), axis=1)
    count = jnp.sum((my_blocks[None, :] == arriving[:, None]).astype(jnp.int32), axis=1)

    slots = jax.ShapeDtypeStruct((slot_total, inner_here), jnp.bfloat16)
    rows = jax.ShapeDtypeStruct((query_total, inner_here), jnp.bfloat16)
    move = 2 * slot_total * query_total * inner_here
    project = 2 * query_total * width * inner_here

    def exchange(x):
        return lax.all_to_all(x, "seq", split_axis=0, concat_axis=0, tiled=True)

    full_grad = lax.all_gather(out_grad, "head", axis=0, tiled=True)
    (send_queries,) = call(send_kernel, [slots], move, local_docs, queries)
    got_queries = exchange(send_queries)
    (send_grads,) = call(
        grad_send_kernel, [slots], move + project, local_docs, full_grad, out_proj
    )
    got_grads = exchange(send_grads)
    far_attended, far_grads, grad_k, grad_v = attend(
        first, count, got_queries, got_grads, enc_keys, enc_values
    )
    back_attended = exchange(far_attended)
    mixed_part, weight_part = call(
        project_kernel,
        [
            jax.ShapeDtypeStruct((query_total, width), jnp.bfloat16),
            jax.ShapeDtypeStruct((inner_here, width), jnp.bfloat16),
        ],
        move + 2 * project,
        local_docs,
        back_attended,
        out_proj,
        full_grad,
    )
    mixed_out = lax.psum_scatter(mixed_part, "head", scatter_dimension=0, tiled=True)
    back_grads = exchange(far_grads)
    (grad_q,) = call(collect_kernel, [rows], move, local_docs, back_grads)
    grad_wo = lax.psum_scatter(weight_part, "seq", scatter_dimension=1, tiled=True).astype(
        jnp.float32
    )
    return (mixed_out, grad_q, grad_k, grad_v, grad_wo)


def solution(mesh):
    placed = (
        P("seq", "head"),
        P("seq", "head"),
        P("seq", "head"),
        P("head", None),
        P(("seq", "head"), None),
        P(),
        P(),
    )
    return jax.shard_map(
        shards,
        mesh=mesh,
        in_specs=placed,
        out_specs=(
            P(("seq", "head"), None),
            P("seq", "head"),
            P("seq", "head"),
            P("seq", "head"),
            P("head", "seq"),
        ),
        check_vma=False,
    )
```

time: 438 us -> 276 us (0.63); the launches traced: 432 us -> 275 us
  matrix products: 196 us -> 0 us
  local copies, waits for them, and re-layouts: 118 us -> 1.97 us
  blocking collectives: 0 us -> 79.9 us
  waiting for transfers between devices: 43.4 us -> 117 us
  Pallas kernels: 0 us -> 49.2 us
  other arithmetic: 40.4 us -> 2.1 us
  starting transfers between devices: 19 us -> 11.2 us
    dot_general x59 -> x0, matrix products: 196 us -> none  [the longest x8 56.7 us: output_step(): jnp.einsum('rhk,khd->rhd', weights, value_block, preferred_element_type=j...]
    all_to_all x0 -> x2, blocking collectives: none -> 79.9 us  [exchange(): return lax.all_to_all(x, 'seq', split_axis=0, concat_axis=0, tiled=True)]
    pallas_call x0 -> x5, Pallas kernels: none -> 49.2 us  [the longest x1 31 us: attend(): pl.pallas_call(attend_kernel, grid_spec=pltpu.PrefetchScalarGridSpec(num_...]
    reduce_scatter x2, waiting for transfers between devices: 0.01 us -> 48.9 us  [the longest x1 48.7 us: shards(): lax.psum_scatter(mixed_part, 'head', scatter_dimension=0, tiled=True)]
    all_gather x1, waiting for transfers between devices: 0.02 us -> 38.2 us  [shards(): full_grad = lax.all_gather(out_grad, 'head', axis=0, tiled=True)]
    scatter x4 -> x0, local copies, waits for them, and re-layouts: 33.2 us -> none  [the longest x2 18.6 us: shards(): jnp.zeros((slot_total, inner_here), jnp.bfloat16).at[source_rows]]
    unnamed x22 -> x8, local copies, waits for them, and re-layouts: 31.9 us -> 1.14 us
    reduce_sum x13 -> x1, other arithmetic: 21.7 us -> 0.18 us  [shards(): jnp.sum((my_blocks[None, :] == arriving[:, None]).astype(jnp.int32), axis=1)]
  transfers between devices with their start and end apart: 7 -> 5, of which waited for: 3 -> 4; matrix products, arithmetic and copies ran while one was open for 66% -> 1% of each run, Pallas kernels for 0% -> 4%
where the time goes in v1:
time: 276 us; the launch traced here: 275 us
  waiting for transfers between devices  117 us (42%)
  blocking collectives  79.9 us (29%)
  Pallas kernels  49.2 us (18%)
  between operations  13.8 us (5%)
  starting transfers between devices  11.2 us (4%)
    all_to_all x2, blocking collectives, exchange(): return lax.all_to_all(x, 'seq', split_axis=0, concat_axis=0, tiled=True)  79.9 us
    reduce_scatter x1, waiting for transfers between devices, shards(): lax.psum_scatter(mixed_part, 'head', scatter_dimension=0, tiled=True)  48.7 us
    all_gather x1, waiting for transfers between devices, shards(): full_grad = lax.all_gather(out_grad, 'head', axis=0, tiled=True)  38.2 us
    pallas_call x1, Pallas kernels, attend(): pl.pallas_call(attend_kernel, grid_spec=pltpu.PrefetchScalarGridSpec(num_...  31 us
    all_to_all x2, waiting for transfers between devices, exchange(): return lax.all_to_all(x, 'seq', split_axis=0, concat_axis=0, tiled=True)  29 us
    pallas_call x4, Pallas kernels, call(): pl.pallas_call(kernel, out_shape=outs, in_specs=[whole] * len(operands),...  18.2 us
    all_to_all x2, starting transfers between devices, exchange(): return lax.all_to_all(x, 'seq', split_axis=0, concat_axis=0, tiled=True)  11.1 us
  transfers between devices with their start and end apart: 5, of which 4 were waited for; matrix products, arithmetic and copies ran while one was open for 1% of the time, Pallas kernels for 4%

profile of v1, /device:TPU:0, one launch (start us, length us, event | category | flops | bytes accessed | tf_op | source)
XLA Modules:
  0.0 275.5 jit_solution(5529467751051079537)
XLA Ops:
  7.2 0.0 all-gather.2.cloned.1.call-start
  7.2 0.7 all-gather.2.cloned.1.call-update
  7.9 0.7 reshape.23
  8.7 0.0 copy-start.2
  8.7 1.1 copy-done.2
  9.8 0.0 copy-start
  9.8 2.3 shard_map.110
  12.1 6.3 %all-to-all-start = ((bf16[8,144,512]{2,1,0:T(8,128)(2,1)}), bf16[8,144,512]{2,1,0:T(8,128)(2,1)S(1)}, u32[]{:S(2)}, u32[]{:S(2)}) async-start(bf16[8,144,512]{2,1,0:T(8,128)(2,1)} %bitcast), calls=%async_computation | async-start | bytes 2359296 | tf_op jit(solution)/shard_map/all_to_all | solution.py:181
  18.4 38.2 %all-gather.2.cloned.1.call-done.grad_ref = bf16[768,2048]{1,0:T(8,128)(2,1)} async-done(((bf16[192,2048]{1,0:T(8,128)(2,1)}), bf16[768,2048]{1,0:T(8,128)(2,1)}) %all-gather.2.cloned.1.call-update) | async-done | bytes 3145744 | tf_op jit(solution)/shard_map/all_gather | solution.py:183
  56.6 0.0 copy-done
  56.6 5.7 %shard_map.111 = bf16[1152,512]{1,0:T(8,128)(2,1)} custom-call(s32[1,768]{1,0:T(1,128)S(1)} %constant_dynamic-slice_fusion.docs_ref, bf16[768,2048]{1,0:T(8,128)(2,1)} %all-gather.2.cloned.1.call-done.grad_ref, bf16[512,2048]{1,0:T(8,128)(2,1)S(1)} %copy-done), custom_call_target="tpu_custom_call" | custom-call | flops 2516582400 | bytes 6425600 | tf_op jit(solution)/shard_map/pallas_call | solution.py:128
  62.3 0.0 copy-start.3
  62.3 0.0 all-to-all-done
  62.3 4.7 %all-to-all-start.1 = ((bf16[8,144,512]{2,1,0:T(8,128)(2,1)}), bf16[8,144,512]{2,1,0:T(8,128)(2,1)S(1)}, u32[]{:S(2)}, u32[]{:S(2)}) async-start(bf16[8,144,512]{2,1,0:T(8,128)(2,1)} %bitcast.2), calls=%async_computation.1 | async-start | bytes 2359296 | tf_op jit(solution)/shard_map/all_to_all | solution.py:181
  67.0 0.0 reduce-scatter.5.cloned.1.call-start
  67.1 0.0 copy-done.3
  67.1 0.1 dynamic_slice.7
  67.1 0.1 select_reduce_fusion
  67.3 0.2 convert_reduce_fusion
  67.5 28.9 %all-to-all-done.1 = bf16[8,144,512]{2,1,0:T(8,128)(2,1)S(1)} async-done(((bf16[8,144,512]{2,1,0:T(8,128)(2,1)}), bf16[8,144,512]{2,1,0:T(8,128)(2,1)S(1)}, u32[]{:S(2)}, u32[]{:S(2)}) %all-to-all-start.1) | async-done | bytes 1179680 | tf_op jit(solution)/shard_map/all_to_all | solution.py:181
  96.4 31.0 %shard_map.112 = (bf16[1152,512]{1,0:T(8,128)(2,1)S(1)}, bf16[1152,512]{1,0:T(8,128)(2,1)S(1)}, bf16[2048,512]{1,0:T(8,128)(2,1)}, bf16[2048,512]{1,0:T(8,128)(2,1)}) custom-call(s32[8]{0:T(128)S(1)} %get-tuple-element.18.first_ref, s32[8]{0:T(128)S(1)} %get-tuple-element.17.count_ref, bf16[1152,512]{1,0:T(8,128)(2,1)S(1)} %bitcast.8, ...), custom_call_target="tpu_custom_call" | custom-call | flops 6039797760 | bytes 16777216 | tf_op jit(solution)/shard_map/pallas_call | solution.py:144
  127.4 0.0 copy-start.1
  127.4 31.9 %all_to_all.44 = bf16[8,144,512]{2,1,0:T(8,128)(2,1)S(1)} all-to-all(bf16[8,144,512]{2,1,0:T(8,128)(2,1)S(1)} %bitcast.11), channel_id=1, replica_groups=mesh['seq'=8,'head'=4] {'seq'}, dimensions={0} | all-to-all | bytes 2359296 | tf_op jit(solution)/shard_map/all_to_all | solution.py:181
  159.3 0.0 copy-done.1
  159.3 7.9 %shard_map.113 = (bf16[768,2048]{1,0:T(8,128)(2,1)}, bf16[512,2048]{1,0:T(8,128)(2,1)}) custom-call(s32[1,768]{1,0:T(1,128)S(1)} %constant_dynamic-slice_fusion.docs_ref, bf16[1152,512]{1,0:T(8,128)(2,1)S(1)} %bitcast.12, bf16[512,2048]{1,0:T(8,128)(2,1)S(1)} %copy-done.1, bf16[768,2048]{1,0:T(8,128)(2,1)} %all-gather.2.cloned.1.call-done.grad_ref), custom_call_target="tpu_custom_call" | custom-call | flops 4127195136 | bytes 11668480 | tf_op jit(solution)/shard_map/pallas_call | solution.py:128
  167.2 0.0 reduce-scatter.5.cloned.1.call-update
  167.3 0.0 reduce-scatter.3.cloned.1.call-start
  167.3 0.7 reduce-scatter.3.cloned.1.call-update
  168.0 48.0 %all_to_all.45 = bf16[8,144,512]{2,1,0:T(8,128)(2,1)S(1)} all-to-all(bf16[8,144,512]{2,1,0:T(8,128)(2,1)S(1)} %bitcast.10), channel_id=1, replica_groups=mesh['seq'=8,'head'=4] {'seq'}, dimensions={0} | all-to-all | bytes 2359296 | tf_op jit(solution)/shard_map/all_to_all | solution.py:181
  216.0 2.3 shard_map.114
  218.3 0.1 reduce-scatter.5.cloned.1.call-done
  218.4 1.8 convert_element_type.11
  220.2 48.7 %reduce-scatter.3.cloned.1.call-done = bf16[192,2048]{1,0:T(8,128)(2,1)} async-done(((bf16[768,2048]{1,0:T(8,128)(2,1)}), bf16[192,2048]{1,0:T(8,128)(2,1)}) %reduce-scatter.3.cloned.1.call-update) | async-done | bytes 786448 | tf_op jit(solution)/shard_map/reduce_scatter | solution.py:206
  (1 shorter events, 0.0 us)
Async XLA Ops:
  7.2 49.4 %all-gather.2.cloned.1.call-start = ((), (), s32[]{:S(2)}) async-start(), calls=%async_computation.6 | async-start | bytes 3932160 | tf_op jit(solution)/shard_map/all_gather | solution.py:183
  8.7 1.1 copy-start.2
  9.8 46.8 %copy-start = (bf16[512,2048]{1,0:T(8,128)(2,1)S(1)}, bf16[512,2048]{1,0:T(8,128)(2,1)}, u32[]{:S(2)}) copy-start(bf16[512,2048]{1,0:T(8,128)(2,1)} %proj_ref.3) | copy-start | bytes 6291460
  12.1 50.2 %all-to-all-start = ((bf16[8,144,512]{2,1,0:T(8,128)(2,1)}), bf16[8,144,512]{2,1,0:T(8,128)(2,1)S(1)}, u32[]{:S(2)}, u32[]{:S(2)}) async-start(bf16[8,144,512]{2,1,0:T(8,128)(2,1)} %bitcast), calls=%async_computation | async-start | bytes 2359296 | tf_op jit(solution)/shard_map/all_to_all | solution.py:181
  62.3 4.8 %copy-start.3 = (s32[128]{0:T(128)S(1)}, s32[128]{0:T(128)}, u32[]{:S(2)}) copy-start(s32[128]{0:T(128)} %param.12) | copy-start | bytes 1540
  62.3 34.1 %all-to-all-start.1 = ((bf16[8,144,512]{2,1,0:T(8,128)(2,1)}), bf16[8,144,512]{2,1,0:T(8,128)(2,1)S(1)}, u32[]{:S(2)}, u32[]{:S(2)}) async-start(bf16[8,144,512]{2,1,0:T(8,128)(2,1)} %bitcast.2), calls=%async_computation.1 | async-start | bytes 2359296 | tf_op jit(solution)/shard_map/all_to_all | solution.py:181
  67.0 151.4 %reduce-scatter.5.cloned.1.call-start = ((), (), s32[]{:S(2)}) async-start(), calls=%async_computation.8 | async-start | bytes 2359296 | tf_op jit(solution)/shard_map/reduce_scatter | solution.py:209
  127.4 31.9 %copy-start.1 = (bf16[512,2048]{1,0:T(8,128)(2,1)S(1)}, bf16[512,2048]{1,0:T(8,128)(2,1)}, u32[]{:S(2)}) copy-start(bf16[512,2048]{1,0:T(8,128)(2,1)} %proj_ref.3) | copy-start | bytes 6291460
  167.3 101.7 %reduce-scatter.3.cloned.1.call-start = ((), (), s32[]{:S(2)}) async-start(), calls=%async_computation.7 | async-start | bytes 3932160 | tf_op jit(solution)/shard_map/reduce_scatter | solution.py:206
Sparse Core Ops, SparseCore 0:
  9.8 46.6 all-gather.1
  167.4 50.9 reduce-scatter.4
  222.0 46.8 reduce-scatter.2

commit v2 on v1

--- a/solution.py
+++ b/solution.py
@@ -76,50 +76,72 @@
     weight_ref[...] = mm(attended, grad_ref[...], TN).astype(jnp.bfloat16)
 
 
-def attend_kernel(first_ref, count_ref, q_ref, g_ref, k_ref, v_ref, att_ref, gq_ref, gk_ref, gv_ref):
+def split(rows):
+    low = lax.broadcasted_iota(jnp.int32, rows.shape, 1) < HD
+    zero = jnp.zeros_like(rows)
+    return jnp.concatenate([jnp.where(low, rows, zero), jnp.where(low, zero, rows)], axis=0)
+
+
+def join(rows):
+    half = rows.shape[0] // 2
+    low = lax.broadcasted_iota(jnp.int32, (half, rows.shape[1]), 1) < HD
+    return jnp.where(low, rows[:half], rows[half:])
+
+
+def probs_of(q2, k):
+    scores = mm(q2, k, NT) * score_scale
+    terms = jnp.exp(scores - jnp.max(scores, axis=1, keepdims=True))
+    return terms * (1.0 / jnp.sum(terms, axis=1, keepdims=True))
+
+
+def by_count(first_ref, count_ref, work):
     slot = pl.program_id(0)
-    count = count_ref[slot]
-    inner = q_ref.shape[1]
-    low = lax.broadcasted_iota(jnp.int32, (QMOST, PAIR), 1) < HD
-
-    @pl.when(count == 0)
+
+    def run(blocks):
+        work(pl.ds(pl.multiple_of(first_ref[slot] * BLOCK, BLOCK), blocks * BLOCK))
+
+    for blocks in range(1, CAP + 1):
+        pl.when(count_ref[slot] == blocks)(functools.partial(run, blocks))
+
+
+def forward_kernel(first_ref, count_ref, q_ref, k_ref, v_ref, att_ref):
+    @pl.when(count_ref[pl.program_id(0)] == 0)
     def _():
         att_ref[...] = jnp.zeros_like(att_ref)
+
+    def work(keys_here):
+        for c in range(q_ref.shape[1] // PAIR):
+            columns = slice(c * PAIR, (c + 1) * PAIR)
+            weights = probs_of(split(q_ref[:, columns]), k_ref[keys_here, columns])
+            attended = mm(weights.astype(jnp.bfloat16), v_ref[keys_here, columns], NN)
+            att_ref[:, columns] = join(attended).astype(jnp.bfloat16)
+
+    by_count(first_ref, count_ref, work)
+
+
+def backward_kernel(
+    first_ref, count_ref, q_ref, g_ref, att_ref, k_ref, v_ref, gq_ref, gk_ref, gv_ref
+):
+    @pl.when(count_ref[pl.program_id(0)] == 0)
+    def _():
         gq_ref[...] = jnp.zeros_like(gq_ref)
 
-    def work(blocks):
-        keys_here = pl.ds(pl.multiple_of(first_ref[slot] * BLOCK, BLOCK), blocks * BLOCK)
-
-        def split(rows):
-            zero = jnp.zeros_like(rows)
-            return jnp.concatenate([jnp.where(low, rows, zero), jnp.where(low, zero, rows)], axis=0)
-
-        def join(rows):
-            return jnp.where(low, rows[:QMOST], rows[QMOST:])
-
-        for c in range(inner // PAIR):
+    def work(keys_here):
+        for c in range(q_ref.shape[1] // PAIR):
             columns = slice(c * PAIR, (c + 1) * PAIR)
             q2 = split(q_ref[:, columns])
             g2 = split(g_ref[:, columns])
             k = k_ref[keys_here, columns]
             v = v_ref[keys_here, columns]
-            scores = mm(q2, k, NT) * score_scale
-            terms = jnp.exp(scores - jnp.max(scores, axis=1, keepdims=True))
-            probs = terms * (1.0 / jnp.sum(terms, axis=1, keepdims=True))
-            weights = probs.astype(jnp.bfloat16)
-            attended = mm(weights, v, NN).astype(jnp.bfloat16)
-            att_ref[:, columns] = join(attended)
-            delta = jnp.sum(
-                g2.astype(jnp.float32) * attended.astype(jnp.float32), axis=1, keepdims=True
-            )
-            dprobs = mm(g2, v, NT)
-            dscores = (probs * (dprobs - delta)).astype(jnp.bfloat16)
+            probs = probs_of(q2, k)
+            gv_ref[keys_here, columns] = mm(probs.astype(jnp.bfloat16), g2, TN).astype(jnp.bfloat16)
+            both = g_ref[:, columns].astype(jnp.float32) * att_ref[:, columns].astype(jnp.float32)
+            delta = jnp.sum(split(both), axis=1, keepdims=True)
+            dscores = (probs * (mm(g2, v, NT) - delta)).astype(jnp.bfloat16)
             gq_ref[:, columns] = join(mm(dscores, k, NN) * score_scale).astype(jnp.bfloat16)
             gk_ref[keys_here, columns] = (mm(dscores, q2, TN) * score_scale).astype(jnp.bfloat16)
-            gv_ref[keys_here, columns] = mm(weights, g2, TN).astype(jnp.bfloat16)
-
-    for blocks in range(1, CAP + 1):
-        pl.when(count == blocks)(functools.partial(work, blocks))
+
+    by_count(first_ref, count_ref, work)
 
 
 def call(kernel, outs, flops, *operands):
@@ -135,26 +157,25 @@
     )(*operands)
 
 
-def attend(first, count, queries, grads, keys, values):
-    slot_total, inner = queries.shape
+def attend(kernel, first, count, row_arrays, key_arrays, outs, flops):
+    slot_total, inner = row_arrays[0].shape
     rows = pl.BlockSpec((QMOST, inner), lambda s, first, count: (s, 0))
-    whole = pl.BlockSpec(keys.shape, lambda s, first, count: (0, 0))
-    shapes = [jax.ShapeDtypeStruct(x.shape, jnp.bfloat16) for x in (queries, queries, keys, keys)]
-    work = slot_total * keys.shape[0] // DPS * inner
+    whole = pl.BlockSpec(key_arrays[0].shape, lambda s, first, count: (0, 0))
+    work = slot_total * key_arrays[0].shape[0] // DPS * inner
     return pl.pallas_call(
-        attend_kernel,
+        kernel,
         grid_spec=pltpu.PrefetchScalarGridSpec(
             num_scalar_prefetch=2,
             grid=(slot_total // QMOST,),
-            in_specs=[rows, rows, whole, whole],
-            out_specs=[rows, rows, whole, whole],
+            in_specs=[rows] * len(row_arrays) + [whole] * len(key_arrays),
+            out_specs=[rows if x.shape == row_arrays[0].shape else whole for x in outs],
         ),
-        out_shape=shapes,
+        out_shape=outs,
         compiler_params=pltpu.CompilerParams(vmem_limit_bytes=VMEM_LIMIT),
         cost_estimate=pl.CostEstimate(
-            flops=40 * work, bytes_accessed=16 * 1024 * 1024, transcendentals=work // HD
+            flops=flops * work, bytes_accessed=16 * 1024 * 1024, transcendentals=work // HD
         ),
-    )(first, count, queries, grads, keys, values)
+    )(first, count, *row_arrays, *key_arrays)
 
 
 def shards(queries, enc_keys, enc_values, out_proj, out_grad, block_doc, query_doc):
@@ -183,14 +204,15 @@
     full_grad = lax.all_gather(out_grad, "head", axis=0, tiled=True)
     (send_queries,) = call(send_kernel, [slots], move, local_docs, queries)
     got_queries = exchange(send_queries)
+    keys = jax.ShapeDtypeStruct(enc_keys.shape, jnp.bfloat16)
+    (far_attended,) = attend(
+        forward_kernel, first, count, [got_queries], [enc_keys, enc_values], [slots], 16
+    )
+    back_attended = exchange(far_attended)
     (send_grads,) = call(
         grad_send_kernel, [slots], move + project, local_docs, full_grad, out_proj
     )
     got_grads = exchange(send_grads)
-    far_attended, far_grads, grad_k, grad_v = attend(
-        first, count, got_queries, got_grads, enc_keys, enc_values
-    )
-    back_attended = exchange(far_attended)
     mixed_part, weight_part = call(
         project_kernel,
         [
@@ -203,8 +225,20 @@
         out_proj,
         full_grad,
     )
-    mixed_out = lax.psum_scatter(mixed_part, "head", scatter_dimension=0, tiled=True)
-    back_grads = exchange(far_grads)
+    back_grads_part, grad_k, grad_v = attend(
+        backward_kernel,
+        first,
+        count,
+        [got_queries, got_grads, far_attended],
+        [enc_keys, enc_values],
+        [slots, keys, keys],
+        32,
+    )
+    back_grads = exchange(back_grads_part)
+    parts = lax.all_to_all(mixed_part, "head", split_axis=0, concat_axis=0, tiled=True)
+    mixed_out = jnp.sum(
+        parts.reshape(lax.axis_size("head"), -1, width).astype(jnp.float32), axis=0
+    ).astype(jnp.bfloat16)
     (grad_q,) = call(collect_kernel, [rows], move, local_docs, back_grads)
     grad_wo = lax.psum_scatter(weight_part, "seq", scatter_dimension=1, tiled=True).astype(
         jnp.float32

time: 276 us -> 213 us (0.77)
  blocking collectives: 79.9 us -> 0 us
  waiting for transfers between devices: 117 us -> 104 us
  starting transfers between devices: 11.2 us -> 21.9 us
  Pallas kernels: 49.2 us -> 58.7 us
  local copies, waits for them, and re-layouts: 1.97 us -> 7.73 us
  other arithmetic: 2.1 us -> 5.69 us
    all_to_all x2 -> x0, blocking collectives: 79.9 us -> none  [exchange(): return lax.all_to_all(x, 'seq', split_axis=0, concat_axis=0, tiled=True)]
    all_to_all x2 -> x4, waiting for transfers between devices: 29 us -> 96.5 us  [exchange(): return lax.all_to_all(x, 'seq', split_axis=0, concat_axis=0, tiled=True)]
    reduce_scatter x1 -> x0, waiting for transfers between devices: 48.7 us -> none  [shards(): lax.psum_scatter(mixed_part, 'head', scatter_dimension=0, tiled=True)]
    all_gather x1, waiting for transfers between devices: 38.2 us -> 0.02 us  [shards(): full_grad = lax.all_gather(out_grad, 'head', axis=0, tiled=True)]
    pallas_call x1 -> x2, Pallas kernels: 31 us -> 41.5 us  [attend(): pl.pallas_call(kernel, grid_spec=pltpu.PrefetchScalarGridSpec(num_scalar_...]
    all_to_all x0 -> x1, waiting for transfers between devices: none -> 6.41 us  [shards(): lax.all_to_all(mixed_part, 'head', split_axis=0, concat_axis=0, tiled=True)]
    all_to_all x2 -> x4, starting transfers between devices: 11.1 us -> 17 us  [exchange(): return lax.all_to_all(x, 'seq', split_axis=0, concat_axis=0, tiled=True)]
    unnamed x8 -> x12, local copies, waits for them, and re-layouts: 1.14 us -> 6.9 us
  transfers between devices with their start and end apart: 5 -> 7, of which waited for: 4 -> 5; matrix products, arithmetic and copies ran while one was open for 1% -> 2% of each run, Pallas kernels for 4% -> 28%
where the time goes in v2:
time: 213 us; the launch traced here: 212 us
  waiting for transfers between devices  104 us (49%)
  Pallas kernels  58.7 us (28%)
  starting transfers between devices  21.9 us (10%)
  between operations  14.1 us (7%)
  local copies, waits for them, and re-layouts  7.73 us (4%)
  other arithmetic  5.69 us (3%)
    all_to_all x4, waiting for transfers between devices, exchange(): return lax.all_to_all(x, 'seq', split_axis=0, concat_axis=0, tiled=True)  96.5 us
    pallas_call x2, Pallas kernels, attend(): pl.pallas_call(kernel, grid_spec=pltpu.PrefetchScalarGridSpec(num_scalar_...  41.5 us
    pallas_call x4, Pallas kernels, call(): pl.pallas_call(kernel, out_shape=outs, in_specs=[whole] * len(operands),...  17.2 us
    all_to_all x4, starting transfers between devices, exchange(): return lax.all_to_all(x, 'seq', split_axis=0, concat_axis=0, tiled=True)  17 us
    unnamed x12, local copies, waits for them, and re-layouts  6.9 us
    all_to_all x1, waiting for transfers between devices, shards(): lax.all_to_all(mixed_part, 'head', split_axis=0, concat_axis=0, tiled=True)  6.41 us
    all_to_all x1, starting transfers between devices, shards(): lax.all_to_all(mixed_part, 'head', split_axis=0, concat_axis=0, tiled=True)  4.65 us
  transfers between devices with their start and end apart: 7, of which 5 were waited for; matrix products, arithmetic and copies ran while one was open for 2% of the time, Pallas kernels for 28%

profile of v2, /device:TPU:0, one launch (start us, length us, event | category | flops | bytes accessed | tf_op | source)
XLA Modules:
  0.0 212.3 jit_solution(6284538636368661851)
XLA Ops:
  7.2 0.0 all-gather.2.cloned.1.call-start
  7.2 0.7 all-gather.2.cloned.1.call-update
  7.9 0.7 reshape.27
  8.7 0.0 copy-start.4
  8.7 1.1 copy-done.4
  9.8 0.0 copy-start.5
  9.8 2.3 %shard_map.110 = bf16[1152,512]{1,0:T(8,128)(2,1)} custom-call(s32[1,768]{1,0:T(1,128)S(1)} %constant_dynamic-slice_fusion.docs_ref, bf16[768,512]{1,0:T(8,128)(2,1)S(1)} %copy-done.4), custom_call_target="tpu_custom_call" | custom-call | flops 905969664 | bytes 1969152 | tf_op jit(solution)/shard_map/pallas_call | solution.py:150
  12.1 6.3 %all-to-all-start = ((bf16[8,144,512]{2,1,0:T(8,128)(2,1)}), bf16[8,144,512]{2,1,0:T(8,128)(2,1)S(1)}, u32[]{:S(2)}, u32[]{:S(2)}) async-start(bf16[8,144,512]{2,1,0:T(8,128)(2,1)} %bitcast), calls=%async_computation | async-start | bytes 2359296 | tf_op jit(solution)/shard_map/all_to_all | solution.py:202
  18.4 0.0 copy-done.5
  18.4 0.1 dynamic_slice.7
  18.5 0.1 select_reduce_fusion
  18.6 0.2 convert_reduce_fusion
  18.8 29.0 %all-to-all-done = bf16[8,144,512]{2,1,0:T(8,128)(2,1)S(1)} async-done(((bf16[8,144,512]{2,1,0:T(8,128)(2,1)}), bf16[8,144,512]{2,1,0:T(8,128)(2,1)S(1)}, u32[]{:S(2)}, u32[]{:S(2)}) %all-to-all-start) | async-done | bytes 1179680 | tf_op jit(solution)/shard_map/all_to_all | solution.py:202
  47.8 0.0 copy-start.3
  47.8 1.6 copy-done.3
  49.4 12.4 %shard_map.111.att_ref = bf16[1152,512]{1,0:T(8,128)(2,1)} custom-call(s32[8]{0:T(128)S(1)} %get-tuple-element.16.first_ref, s32[8]{0:T(128)S(1)} %get-tuple-element.15.count_ref, bf16[1152,512]{1,0:T(8,128)(2,1)S(1)} %bitcast.9, bf16[2048,512]{1,0:T(8,128)(2,1)S(1)} %copy-done.3, bf16[2048,512]{1,0:T(8,128)(2,1)} %v_ref.3), custom_call_target="tpu_custom_call" | custom-call | flops 2415919104 | bytes 16777216 | tf_op jit(solution)/shard_map/pallas_call | solution.py:165
  61.8 3.6 %all-to-all-start.1 = ((bf16[8,144,512]{2,1,0:T(8,128)(2,1)}), bf16[8,144,512]{2,1,0:T(8,128)(2,1)S(1)}, u32[]{:S(2)}, u32[]{:S(2)}) async-start(bf16[8,144,512]{2,1,0:T(8,128)(2,1)} %bitcast.2), calls=%async_computation.1 | async-start | bytes 2359296 | tf_op jit(solution)/shard_map/all_to_all | solution.py:202
  65.4 0.0 all-gather.2.cloned.1.call-done.grad_ref
  65.4 0.0 copy-start.1
  65.4 1.6 copy-done.1
  67.0 4.7 %shard_map.113 = bf16[1152,512]{1,0:T(8,128)(2,1)S(1)} custom-call(s32[1,768]{1,0:T(1,128)S(1)} %constant_dynamic-slice_fusion.docs_ref, bf16[768,2048]{1,0:T(8,128)(2,1)} %all-gather.2.cloned.1.call-done.grad_ref, bf16[512,2048]{1,0:T(8,128)(2,1)S(1)} %copy-done.1), custom_call_target="tpu_custom_call" | custom-call | flops 2516582400 | bytes 6425600 | tf_op jit(solution)/shard_map/pallas_call | solution.py:150
  71.7 0.0 copy-start
  71.7 1.0 copy-done
  72.8 22.0 %all-to-all-done.1 = bf16[8,144,512]{2,1,0:T(8,128)(2,1)S(1)} async-done(((bf16[8,144,512]{2,1,0:T(8,128)(2,1)}), bf16[8,144,512]{2,1,0:T(8,128)(2,1)S(1)}, u32[]{:S(2)}, u32[]{:S(2)}) %all-to-all-start.1) | async-done | bytes 1179680 | tf_op jit(solution)/shard_map/all_to_all | solution.py:202
  94.7 3.6 %all-to-all-start.3 = ((bf16[8,144,512]{2,1,0:T(8,128)(2,1)}), bf16[8,144,512]{2,1,0:T(8,128)(2,1)S(1)}, u32[]{:S(2)}, u32[]{:S(2)}) async-start(bf16[8,144,512]{2,1,0:T(8,128)(2,1)} %bitcast.13), calls=%async_computation.3 | async-start | bytes 2359296 | tf_op jit(solution)/shard_map/all_to_all | solution.py:202
  98.3 0.0 copy-start.2
  98.3 1.6 copy-done.2
  99.9 7.9 %shard_map.112 = (bf16[768,2048]{1,0:T(8,128)(2,1)}, bf16[512,2048]{1,0:T(8,128)(2,1)}) custom-call(s32[1,768]{1,0:T(1,128)S(1)} %constant_dynamic-slice_fusion.docs_ref, bf16[1152,512]{1,0:T(8,128)(2,1)S(1)} %bitcast.12, bf16[512,2048]{1,0:T(8,128)(2,1)S(1)} %copy-done.2, bf16[768,2048]{1,0:T(8,128)(2,1)} %all-gather.2.cloned.1.call-done.grad_ref), custom_call_target="tpu_custom_call" | custom-call | flops 4127195136 | bytes 11668480 | tf_op jit(solution)/shard_map/pallas_call | solution.py:150
  107.8 19.8 %all-to-all-done.3 = bf16[8,144,512]{2,1,0:T(8,128)(2,1)S(1)} async-done(((bf16[8,144,512]{2,1,0:T(8,128)(2,1)}), bf16[8,144,512]{2,1,0:T(8,128)(2,1)S(1)}, u32[]{:S(2)}, u32[]{:S(2)}) %all-to-all-start.3) | async-done | bytes 1179680 | tf_op jit(solution)/shard_map/all_to_all | solution.py:202
  127.6 4.7 %all-to-all-start.2 = ((bf16[4,192,2048]{2,1,0:T(8,128)(2,1)}), bf16[4,192,2048]{2,1,0:T(8,128)(2,1)}, u32[]{:S(2)}, u32[]{:S(2)}) async-start(bf16[4,192,2048]{2,1,0:T(8,128)(2,1)} %bitcast.15), calls=%async_computation.2 | async-start | bytes 6291456 | tf_op jit(solution)/shard_map/all_to_all | solution.py:238
  132.3 0.2 reduce-scatter.2.cloned.1.call-start
  132.5 0.5 reduce-scatter.2.cloned.1.call-update
  133.0 29.1 %shard_map.114 = (bf16[1152,512]{1,0:T(8,128)(2,1)}, bf16[2048,512]{1,0:T(8,128)(2,1)}, bf16[2048,512]{1,0:T(8,128)(2,1)}) custom-call(s32[8]{0:T(128)S(1)} %get-tuple-element.16.first_ref, s32[8]{0:T(128)S(1)} %get-tuple-element.15.count_ref, bf16[1152,512]{1,0:T(8,128)(2,1)S(1)} %bitcast.10, bf16[1152,512]{1,0:T(8,128)(2,1)S(1)} %bitcast.11, ...), custom_call_target="tpu_custom_call" | custom-call | flops 4831838208 | bytes 16777216 | tf_op jit(solution)/shard_map/pallas_call | solution.py:165
  162.1 6.4 %all-to-all-done.2 = bf16[4,192,2048]{2,1,0:T(8,128)(2,1)} async-done(((bf16[4,192,2048]{2,1,0:T(8,128)(2,1)}), bf16[4,192,2048]{2,1,0:T(8,128)(2,1)}, u32[]{:S(2)}, u32[]{:S(2)}) %all-to-all-start.2) | async-done | bytes 3145760 | tf_op jit(solution)/shard_map/all_to_all | solution.py:238
  168.5 3.6 %all-to-all-start.4 = ((bf16[8,144,512]{2,1,0:T(8,128)(2,1)}), bf16[8,144,512]{2,1,0:T(8,128)(2,1)S(1)}, u32[]{:S(2)}, u32[]{:S(2)}) async-start(bf16[8,144,512]{2,1,0:T(8,128)(2,1)} %bitcast.7), calls=%async_computation.4 | async-start | bytes 2359296 | tf_op jit(solution)/shard_map/all_to_all | solution.py:202
  172.1 3.6 %reduce_sum.32 = bf16[192,2048]{1,0:T(8,128)(2,1)} reduce(bf16[4,192,2048]{2,1,0:T(8,128)(2,1)} %all-to-all-done.2, bf16[]{:T(256)} %constant.33.clone.1), dimensions={0}, to_apply=%region_3.4 | reduce | flops 1179648 | bytes 3932162 | tf_op jit(solution)/shard_map/reduce_sum | solution.py:239
  175.7 25.7 %all-to-all-done.4 = bf16[8,144,512]{2,1,0:T(8,128)(2,1)S(1)} async-done(((bf16[8,144,512]{2,1,0:T(8,128)(2,1)}), bf16[8,144,512]{2,1,0:T(8,128)(2,1)S(1)}, u32[]{:S(2)}, u32[]{:S(2)}) %all-to-all-start.4) | async-done | bytes 1179680 | tf_op jit(solution)/shard_map/all_to_all | solution.py:202
  201.4 2.3 %shard_map.115 = bf16[768,512]{1,0:T(8,128)(2,1)} custom-call(s32[1,768]{1,0:T(1,128)S(1)} %constant_dynamic-slice_fusion.docs_ref, bf16[1152,512]{1,0:T(8,128)(2,1)S(1)} %bitcast.14), custom_call_target="tpu_custom_call" | custom-call | flops 905969664 | bytes 1969152 | tf_op jit(solution)/shard_map/pallas_call | solution.py:150
  203.7 0.0 reduce-scatter.2.cloned.1.call-done
  203.7 1.8 convert_element_type.13
  (1 shorter events, 0.0 us)
Async XLA Ops:
  7.2 58.3 %all-gather.2.cloned.1.call-start = ((), (), s32[]{:S(2)}) async-start(), calls=%async_computation.6 | async-start | bytes 3932160 | tf_op jit(solution)/shard_map/all_gather | solution.py:204
  8.7 1.1 copy-start.4
  9.8 8.6 %copy-start.5 = (s32[128]{0:T(128)S(1)}, s32[128]{0:T(128)}, u32[]{:S(2)}) copy-start(s32[128]{0:T(128)} %param.12) | copy-start | bytes 1540
  12.1 35.7 %all-to-all-start = ((bf16[8,144,512]{2,1,0:T(8,128)(2,1)}), bf16[8,144,512]{2,1,0:T(8,128)(2,1)S(1)}, u32[]{:S(2)}, u32[]{:S(2)}) async-start(bf16[8,144,512]{2,1,0:T(8,128)(2,1)} %bitcast), calls=%async_computation | async-start | bytes 2359296 | tf_op jit(solution)/shard_map/all_to_all | solution.py:202
  47.8 1.6 copy-start.3
  61.8 32.9 %all-to-all-start.1 = ((bf16[8,144,512]{2,1,0:T(8,128)(2,1)}), bf16[8,144,512]{2,1,0:T(8,128)(2,1)S(1)}, u32[]{:S(2)}, u32[]{:S(2)}) async-start(bf16[8,144,512]{2,1,0:T(8,128)(2,1)} %bitcast.2), calls=%async_computation.1 | async-start | bytes 2359296 | tf_op jit(solution)/shard_map/all_to_all | solution.py:202
  65.4 1.6 copy-start.1
  71.7 1.0 copy-start
  94.7 32.9 %all-to-all-start.3 = ((bf16[8,144,512]{2,1,0:T(8,128)(2,1)}), bf16[8,144,512]{2,1,0:T(8,128)(2,1)S(1)}, u32[]{:S(2)}, u32[]{:S(2)}) async-start(bf16[8,144,512]{2,1,0:T(8,128)(2,1)} %bitcast.13), calls=%async_computation.3 | async-start | bytes 2359296 | tf_op jit(solution)/shard_map/all_to_all | solution.py:202
  98.3 1.6 copy-start.2
  127.6 40.9 %all-to-all-start.2 = ((bf16[4,192,2048]{2,1,0:T(8,128)(2,1)}), bf16[4,192,2048]{2,1,0:T(8,128)(2,1)}, u32[]{:S(2)}, u32[]{:S(2)}) async-start(bf16[4,192,2048]{2,1,0:T(8,128)(2,1)} %bitcast.15), calls=%async_computation.2 | async-start | bytes 6291456 | tf_op jit(solution)/shard_map/all_to_all | solution.py:238
  132.3 71.4 %reduce-scatter.2.cloned.1.call-start = ((), (), s32[]{:S(2)}) async-start(), calls=%async_computation.7 | async-start | bytes 2359296 | tf_op jit(solution)/shard_map/reduce_scatter | solution.py:243
  168.5 32.9 %all-to-all-start.4 = ((bf16[8,144,512]{2,1,0:T(8,128)(2,1)}), bf16[8,144,512]{2,1,0:T(8,128)(2,1)S(1)}, u32[]{:S(2)}, u32[]{:S(2)}) async-start(bf16[8,144,512]{2,1,0:T(8,128)(2,1)} %bitcast.7), calls=%async_computation.4 | async-start | bytes 2359296 | tf_op jit(solution)/shard_map/all_to_all | solution.py:202
Sparse Core Ops, SparseCore 0:
  9.8 46.7 all-gather.1
  135.4 34.9 reduce-scatter.1

commit v3 on v2

--- a/solution.py
+++ b/solution.py
@@ -13,7 +13,7 @@
 DPS = 8
 CAP = 3
 QMOST = 144
-PAIR = 2 * HD
+GROUP = 4 * HD
 VMEM_LIMIT = 48 * 1024 * 1024
 
 score_scale = 0.125
@@ -77,21 +77,32 @@
 
 
 def split(rows):
-    low = lax.broadcasted_iota(jnp.int32, rows.shape, 1) < HD
+    head = lax.broadcasted_iota(jnp.int32, rows.shape, 1) // HD
     zero = jnp.zeros_like(rows)
-    return jnp.concatenate([jnp.where(low, rows, zero), jnp.where(low, zero, rows)], axis=0)
+    return jnp.concatenate(
+        [jnp.where(head == h, rows, zero) for h in range(rows.shape[1] // HD)], axis=0
+    )
 
 
 def join(rows):
-    half = rows.shape[0] // 2
-    low = lax.broadcasted_iota(jnp.int32, (half, rows.shape[1]), 1) < HD
-    return jnp.where(low, rows[:half], rows[half:])
-
-
-def probs_of(q2, k):
-    scores = mm(q2, k, NT) * score_scale
-    terms = jnp.exp(scores - jnp.max(scores, axis=1, keepdims=True))
-    return terms * (1.0 / jnp.sum(terms, axis=1, keepdims=True))
+    heads = rows.shape[1] // HD
+    count = rows.shape[0] // heads
+    head = lax.broadcasted_iota(jnp.int32, (count, rows.shape[1]), 1) // HD
+    joined = rows[:count]
+    for h in range(1, heads):
+        joined = jnp.where(head == h, rows[h * count : (h + 1) * count], joined)
+    return joined
+
+
+def groups(inner):
+    width = min(GROUP, inner)
+    return [slice(c, c + width) for c in range(0, inner, width)]
+
+
+def probs_of(rows, k):
+    scores = mm(k, rows, NT) * score_scale
+    terms = jnp.exp(scores - jnp.max(scores, axis=0, keepdims=True))
+    return terms * (1.0 / jnp.sum(terms, axis=0, keepdims=True))
 
 
 def by_count(first_ref, count_ref, work):
@@ -110,36 +121,34 @@
         att_ref[...] = jnp.zeros_like(att_ref)
 
     def work(keys_here):
-        for c in range(q_ref.shape[1] // PAIR):
-            columns = slice(c * PAIR, (c + 1) * PAIR)
+        for columns in groups(q_ref.shape[1]):
             weights = probs_of(split(q_ref[:, columns]), k_ref[keys_here, columns])
-            attended = mm(weights.astype(jnp.bfloat16), v_ref[keys_here, columns], NN)
+            attended = mm(weights.astype(jnp.bfloat16), v_ref[keys_here, columns], TN)
             att_ref[:, columns] = join(attended).astype(jnp.bfloat16)
 
     by_count(first_ref, count_ref, work)
 
 
-def backward_kernel(
-    first_ref, count_ref, q_ref, g_ref, att_ref, k_ref, v_ref, gq_ref, gk_ref, gv_ref
-):
+def backward_kernel(first_ref, count_ref, q_ref, g_ref, k_ref, v_ref, gq_ref, gk_ref, gv_ref):
     @pl.when(count_ref[pl.program_id(0)] == 0)
     def _():
         gq_ref[...] = jnp.zeros_like(gq_ref)
 
     def work(keys_here):
-        for c in range(q_ref.shape[1] // PAIR):
-            columns = slice(c * PAIR, (c + 1) * PAIR)
-            q2 = split(q_ref[:, columns])
-            g2 = split(g_ref[:, columns])
+        for columns in groups(q_ref.shape[1]):
+            rows = split(q_ref[:, columns])
+            grads = split(g_ref[:, columns])
             k = k_ref[keys_here, columns]
             v = v_ref[keys_here, columns]
-            probs = probs_of(q2, k)
-            gv_ref[keys_here, columns] = mm(probs.astype(jnp.bfloat16), g2, TN).astype(jnp.bfloat16)
-            both = g_ref[:, columns].astype(jnp.float32) * att_ref[:, columns].astype(jnp.float32)
-            delta = jnp.sum(split(both), axis=1, keepdims=True)
-            dscores = (probs * (mm(g2, v, NT) - delta)).astype(jnp.bfloat16)
-            gq_ref[:, columns] = join(mm(dscores, k, NN) * score_scale).astype(jnp.bfloat16)
-            gk_ref[keys_here, columns] = (mm(dscores, q2, TN) * score_scale).astype(jnp.bfloat16)
+            probs = probs_of(rows, k)
+            gv_ref[keys_here, columns] = mm(probs.astype(jnp.bfloat16), grads, NN).astype(
+                jnp.bfloat16
+            )
+            dprobs = mm(v, grads, NT)
+            delta = jnp.sum(probs * dprobs, axis=0, keepdims=True)
+            dscores = (probs * (dprobs - delta)).astype(jnp.bfloat16)
+            gk_ref[keys_here, columns] = (mm(dscores, rows, NN) * score_scale).astype(jnp.bfloat16)
+            gq_ref[:, columns] = join(mm(dscores, k, TN) * score_scale).astype(jnp.bfloat16)
 
     by_count(first_ref, count_ref, work)
 
@@ -229,16 +238,21 @@
         backward_kernel,
         first,
         count,
-        [got_queries, got_grads, far_attended],
+        [got_queries, got_grads],
         [enc_keys, enc_values],
         [slots, keys, keys],
         32,
     )
     back_grads = exchange(back_grads_part)
-    parts = lax.all_to_all(mixed_part, "head", split_axis=0, concat_axis=0, tiled=True)
-    mixed_out = jnp.sum(
-        parts.reshape(lax.axis_size("head"), -1, width).astype(jnp.float32), axis=0
-    ).astype(jnp.bfloat16)
+    head_count = lax.axis_size("head")
+    my_head = lax.axis_index("head")
+    pieces = mixed_part.reshape(head_count, -1, width)
+    total = lax.dynamic_index_in_dim(pieces, my_head, 0, False).astype(jnp.float32)
+    for step in range(1, head_count):
+        piece = lax.dynamic_index_in_dim(pieces, (my_head + step) % head_count, 0, False)
+        pairs = [(i, (i + step) % head_count) for i in range(head_count)]
+        total = total + lax.ppermute(piece, "head", pairs).astype(jnp.float32)
+    mixed_out = total.astype(jnp.bfloat16)
     (grad_q,) = call(collect_kernel, [rows], move, local_docs, back_grads)
     grad_wo = lax.psum_scatter(weight_part, "seq", scatter_dimension=1, tiled=True).astype(
         jnp.float32

time: 213 us -> 214 us (level)
  Pallas kernels: 58.7 us -> 48.8 us
  waiting for transfers between devices: 104 us -> 113 us
    ppermute x0 -> x3, waiting for transfers between devices: none -> 33.4 us  [shards(): total = total + lax.ppermute(piece, 'head', pairs).astype(jnp.float32)]
    all_to_all x4, waiting for transfers between devices: 96.5 us -> 79.3 us  [exchange(): return lax.all_to_all(x, 'seq', split_axis=0, concat_axis=0, tiled=True)]
    pallas_call x2, Pallas kernels: 41.5 us -> 30.6 us  [attend(): pl.pallas_call(kernel, grid_spec=pltpu.PrefetchScalarGridSpec(num_scalar_...]
    all_to_all x1 -> x0, waiting for transfers between devices: 6.41 us -> none  [shards(): lax.all_to_all(mixed_part, 'head', split_axis=0, concat_axis=0, tiled=True)]
    all_to_all x1 -> x0, starting transfers between devices: 4.65 us -> none  [shards(): lax.all_to_all(mixed_part, 'head', split_axis=0, concat_axis=0, tiled=True)]
    ppermute x0 -> x3, starting transfers between devices: none -> 4.44 us  [shards(): total = total + lax.ppermute(piece, 'head', pairs).astype(jnp.float32)]
    reduce_sum x1 -> x0, other arithmetic: 3.59 us -> none  [shards(): jnp.sum(parts.reshape(lax.axis_size('head'), -1, width).astype(jnp.float3...]
    squeeze x0 -> x1, local copies, waits for them, and re-layouts: none -> 3.09 us  [shards(): lax.dynamic_index_in_dim(pieces, (my_head + step) % head_count, 0, False)]
  transfers between devices with their start and end apart: 7 -> 9, of which waited for: 5 -> 5; matrix products, arithmetic and copies ran while one was open for 2% -> 3% of each run, Pallas kernels for 28% -> 23%
where the time goes in v3:
time: 214 us; the launch traced here: 213 us
  waiting for transfers between devices  113 us (53%)
  Pallas kernels  48.8 us (23%)
  starting transfers between devices  21.9 us (10%)
  between operations  14.2 us (7%)
  local copies, waits for them, and re-layouts  9.83 us (5%)
  other arithmetic  4.61 us (2%)
    all_to_all x4, waiting for transfers between devices, exchange(): return lax.all_to_all(x, 'seq', split_axis=0, concat_axis=0, tiled=True)  79.3 us
    ppermute x3, waiting for transfers between devices, shards(): total = total + lax.ppermute(piece, 'head', pairs).astype(jnp.float32)  33.4 us
    pallas_call x2, Pallas kernels, attend(): pl.pallas_call(kernel, grid_spec=pltpu.PrefetchScalarGridSpec(num_scalar_...  30.6 us
    pallas_call x4, Pallas kernels, call(): pl.pallas_call(kernel, out_shape=outs, in_specs=[whole] * len(operands),...  18.2 us
    all_to_all x4, starting transfers between devices, exchange(): return lax.all_to_all(x, 'seq', split_axis=0, concat_axis=0, tiled=True)  17.2 us
    unnamed x12, local copies, waits for them, and re-layouts  5.91 us
    ppermute x3, starting transfers between devices, shards(): total = total + lax.ppermute(piece, 'head', pairs).astype(jnp.float32)  4.44 us
  transfers between devices with their start and end apart: 9, of which 5 were waited for; matrix products, arithmetic and copies ran while one was open for 3% of the time, Pallas kernels for 23%

profile of v3, /device:TPU:0, one launch (start us, length us, event | category | flops | bytes accessed | tf_op | source)
XLA Modules:
  0.0 212.7 jit_solution(12218879825208372402)
XLA Ops:
  7.2 0.0 all-gather.2.cloned.1.call-start
  7.2 0.7 all-gather.2.cloned.1.call-update
  7.9 0.7 reshape.28
  8.7 0.0 copy-start.4
  8.7 1.1 copy-done.4
  9.8 2.3 %shard_map.110 = bf16[1152,512]{1,0:T(8,128)(2,1)} custom-call(s32[1,768]{1,0:T(1,128)S(1)} %constant_dynamic-slice_fusion.docs_ref, bf16[768,512]{1,0:T(8,128)(2,1)S(1)} %copy-done.4), custom_call_target="tpu_custom_call" | custom-call | flops 905969664 | bytes 1969152 | tf_op jit(solution)/shard_map/pallas_call | solution.py:159
  12.1 0.0 copy-start.5
  12.1 0.0 copy-start.2
  12.1 6.5 %all-to-all-start = ((bf16[8,144,512]{2,1,0:T(8,128)(2,1)}), bf16[8,144,512]{2,1,0:T(8,128)(2,1)S(1)}, u32[]{:S(2)}, u32[]{:S(2)}) async-start(bf16[8,144,512]{2,1,0:T(8,128)(2,1)} %bitcast), calls=%async_computation | async-start | bytes 2359296 | tf_op jit(solution)/shard_map/all_to_all | solution.py:211
  18.5 0.0 copy-done.5
  18.5 0.1 dynamic_slice.20
  18.6 0.1 select_reduce_fusion
  18.7 0.2 convert_reduce_fusion
  18.9 29.0 %all-to-all-done = bf16[8,144,512]{2,1,0:T(8,128)(2,1)S(1)} async-done(((bf16[8,144,512]{2,1,0:T(8,128)(2,1)}), bf16[8,144,512]{2,1,0:T(8,128)(2,1)S(1)}, u32[]{:S(2)}, u32[]{:S(2)}) %all-to-all-start) | async-done | bytes 1179680 | tf_op jit(solution)/shard_map/all_to_all | solution.py:211
  47.9 0.0 copy-done.2
  47.9 11.8 %shard_map.111 = bf16[1152,512]{1,0:T(8,128)(2,1)} custom-call(s32[8]{0:T(128)S(1)} %get-tuple-element.16.first_ref, s32[8]{0:T(128)S(1)} %get-tuple-element.15.count_ref, bf16[1152,512]{1,0:T(8,128)(2,1)S(1)} %bitcast.19, bf16[2048,512]{1,0:T(8,128)(2,1)S(1)} %copy-done.2, bf16[2048,512]{1,0:T(8,128)(2,1)} %v_ref.3), custom_call_target="tpu_custom_call" | custom-call | flops 2415919104 | bytes 16777216 | tf_op jit(solution)/shard_map/pallas_call | solution.py:174
  59.7 3.6 %all-to-all-start.1 = ((bf16[8,144,512]{2,1,0:T(8,128)(2,1)}), bf16[8,144,512]{2,1,0:T(8,128)(2,1)S(1)}, u32[]{:S(2)}, u32[]{:S(2)}) async-start(bf16[8,144,512]{2,1,0:T(8,128)(2,1)} %bitcast.2), calls=%async_computation.1 | async-start | bytes 2359296 | tf_op jit(solution)/shard_map/all_to_all | solution.py:211
  63.3 0.0 all-gather.2.cloned.1.call-done.grad_ref
  63.3 0.0 copy-start
  63.3 1.6 copy-done
  64.9 5.7 %shard_map.113 = bf16[1152,512]{1,0:T(8,128)(2,1)} custom-call(s32[1,768]{1,0:T(1,128)S(1)} %constant_dynamic-slice_fusion.docs_ref, bf16[768,2048]{1,0:T(8,128)(2,1)} %all-gather.2.cloned.1.call-done.grad_ref, bf16[512,2048]{1,0:T(8,128)(2,1)S(1)} %copy-done), custom_call_target="tpu_custom_call" | custom-call | flops 2516582400 | bytes 6425600 | tf_op jit(solution)/shard_map/pallas_call | solution.py:159
  70.6 22.0 %all-to-all-done.1 = bf16[8,144,512]{2,1,0:T(8,128)(2,1)S(1)} async-done(((bf16[8,144,512]{2,1,0:T(8,128)(2,1)}), bf16[8,144,512]{2,1,0:T(8,128)(2,1)S(1)}, u32[]{:S(2)}, u32[]{:S(2)}) %all-to-all-start.1) | async-done | bytes 1179680 | tf_op jit(solution)/shard_map/all_to_all | solution.py:211
  92.6 3.6 %all-to-all-start.2 = ((bf16[8,144,512]{2,1,0:T(8,128)(2,1)}), bf16[8,144,512]{2,1,0:T(8,128)(2,1)S(1)}, u32[]{:S(2)}, u32[]{:S(2)}) async-start(bf16[8,144,512]{2,1,0:T(8,128)(2,1)} %bitcast.9), calls=%async_computation.2 | async-start | bytes 2359296 | tf_op jit(solution)/shard_map/all_to_all | solution.py:211
  96.2 0.2 reduce-scatter.2.cloned.1.call-start
  96.4 0.0 copy-start.1
  96.4 1.6 copy-done.1
  98.0 7.9 %shard_map.112 = (bf16[768,2048]{1,0:T(8,128)(2,1)}, bf16[512,2048]{1,0:T(8,128)(2,1)}) custom-call(s32[1,768]{1,0:T(1,128)S(1)} %constant_dynamic-slice_fusion.docs_ref, bf16[1152,512]{1,0:T(8,128)(2,1)S(1)} %bitcast.22, bf16[512,2048]{1,0:T(8,128)(2,1)S(1)} %copy-done.1, bf16[768,2048]{1,0:T(8,128)(2,1)} %all-gather.2.cloned.1.call-done.grad_ref), custom_call_target="tpu_custom_call" | custom-call | flops 4127195136 | bytes 11668480 | tf_op jit(solution)/shard_map/pallas_call | solution.py:159
  105.9 0.0 reduce-scatter.2.cloned.1.call-update
  106.0 28.3 %all-to-all-done.2 = bf16[8,144,512]{2,1,0:T(8,128)(2,1)S(1)} async-done(((bf16[8,144,512]{2,1,0:T(8,128)(2,1)}), bf16[8,144,512]{2,1,0:T(8,128)(2,1)S(1)}, u32[]{:S(2)}, u32[]{:S(2)}) %all-to-all-start.2) | async-done | bytes 1179680 | tf_op jit(solution)/shard_map/all_to_all | solution.py:211
  134.3 0.0 copy-start.3
  134.3 1.6 copy-done.3
  135.9 18.8 %shard_map.114 = (bf16[1152,512]{1,0:T(8,128)(2,1)}, bf16[2048,512]{1,0:T(8,128)(2,1)}, bf16[2048,512]{1,0:T(8,128)(2,1)}) custom-call(s32[8]{0:T(128)S(1)} %get-tuple-element.16.first_ref, s32[8]{0:T(128)S(1)} %get-tuple-element.15.count_ref, bf16[1152,512]{1,0:T(8,128)(2,1)S(1)} %bitcast.20, bf16[1152,512]{1,0:T(8,128)(2,1)S(1)} %bitcast.21, ...), custom_call_target="tpu_custom_call" | custom-call | flops 4831838208 | bytes 16777216 | tf_op jit(solution)/shard_map/pallas_call | solution.py:174
  154.7 3.6 %all-to-all-start.3 = ((bf16[8,144,512]{2,1,0:T(8,128)(2,1)}), bf16[8,144,512]{2,1,0:T(8,128)(2,1)S(1)}, u32[]{:S(2)}, u32[]{:S(2)}) async-start(bf16[8,144,512]{2,1,0:T(8,128)(2,1)} %bitcast.11), calls=%async_computation.3 | async-start | bytes 2359296 | tf_op jit(solution)/shard_map/all_to_all | solution.py:211
  158.3 3.1 %dynamic-slice_bitcast_fusion.2 = (bf16[192,2048]{1,0:T(8,128)(2,1)}, bf16[192,2048]{1,0:T(8,128)(2,1)}, bf16[192,2048]{1,0:T(8,128)(2,1)}) fusion(bf16[4,192,2048]{2,1,0:T(8,128)(2,1)} %bitcast.23, s32[]{:T(128)S(6)} %select_n.49, s32[]{:T(128)S(6)} %select_n.53, s32[]{:T(128)S(6)} %select_n.51), kind=kLoop, calls=%fused_computation.6 | loop fusion | bytes 4718604 | tf_op jit(solution)/shard_map/jit(dynamic_index_in_dim)/squeeze | solution.py:252
  161.4 1.5 collective-permute-start
  162.9 1.4 collective-permute-start.2
  164.3 1.5 collective-permute-start.1
  165.8 17.1 %collective-permute-done = bf16[192,2048]{1,0:T(8,128)(2,1)S(1)} collective-permute-done((bf16[192,2048]{1,0:T(8,128)(2,1)}, bf16[192,2048]{1,0:T(8,128)(2,1)S(1)}, u32[]{:S(2)}, u32[]{:S(2)}) %collective-permute-start) | collective-permute-done | bytes 786464 | tf_op jit(solution)/shard_map/ppermute | solution.py:254
  182.9 16.3 %collective-permute-done.2 = bf16[192,2048]{1,0:T(8,128)(2,1)S(1)} collective-permute-done((bf16[192,2048]{1,0:T(8,128)(2,1)}, bf16[192,2048]{1,0:T(8,128)(2,1)S(1)}, u32[]{:S(2)}, u32[]{:S(2)}) %collective-permute-start.2) | collective-permute-done | bytes 786464 | tf_op jit(solution)/shard_map/ppermute | solution.py:254
  199.3 0.0 collective-permute-done.1
  199.3 2.5 %fusion.2 = bf16[192,2048]{1,0:T(8,128)(2,1)} fusion(bf16[192,2048]{1,0:T(8,128)(2,1)S(1)} %collective-permute-done.2, bf16[192,2048]{1,0:T(8,128)(2,1)S(1)} %collective-permute-done.1, bf16[192,2048]{1,0:T(8,128)(2,1)S(1)} %collective-permute-done, bf16[4,192,2048]{2,1,0:T(8,128)(2,1)} %bitcast.24, s32[]{:T(128)S(6)} %select_n.47), kind=kLoop, calls=%fused_computation.3 | loop fusion | flops 3145728 | bytes 3932164 | tf_op jit(solution)/shard_map/convert_element_type | solution.py:255
  201.8 0.0 all-to-all-done.3
  201.8 2.3 %shard_map.115 = bf16[768,512]{1,0:T(8,128)(2,1)} custom-call(s32[1,768]{1,0:T(1,128)S(1)} %constant_dynamic-slice_fusion.docs_ref, bf16[1152,512]{1,0:T(8,128)(2,1)S(1)} %bitcast.18), custom_call_target="tpu_custom_call" | custom-call | flops 905969664 | bytes 1969152 | tf_op jit(solution)/shard_map/pallas_call | solution.py:159
  204.1 0.0 reduce-scatter.2.cloned.1.call-done
  204.1 1.8 convert_element_type.35
  (1 shorter events, 0.0 us)
Async XLA Ops:
  7.2 56.2 %all-gather.2.cloned.1.call-start = ((), (), s32[]{:S(2)}) async-start(), calls=%async_computation.5 | async-start | bytes 3932160 | tf_op jit(solution)/shard_map/all_gather | solution.py:213
  8.7 1.1 copy-start.4
  12.1 6.5 %copy-start.5 = (s32[128]{0:T(128)S(1)}, s32[128]{0:T(128)}, u32[]{:S(2)}) copy-start(s32[128]{0:T(128)} %param.12) | copy-start | bytes 1540
  12.1 35.9 %copy-start.2 = (bf16[2048,512]{1,0:T(8,128)(2,1)S(1)}, bf16[2048,512]{1,0:T(8,128)(2,1)}, u32[]{:S(2)}) copy-start(bf16[2048,512]{1,0:T(8,128)(2,1)} %k_ref.3) | copy-start | bytes 6291460
  12.1 35.9 %all-to-all-start = ((bf16[8,144,512]{2,1,0:T(8,128)(2,1)}), bf16[8,144,512]{2,1,0:T(8,128)(2,1)S(1)}, u32[]{:S(2)}, u32[]{:S(2)}) async-start(bf16[8,144,512]{2,1,0:T(8,128)(2,1)} %bitcast), calls=%async_computation | async-start | bytes 2359296 | tf_op jit(solution)/shard_map/all_to_all | solution.py:211
  59.7 32.9 %all-to-all-start.1 = ((bf16[8,144,512]{2,1,0:T(8,128)(2,1)}), bf16[8,144,512]{2,1,0:T(8,128)(2,1)S(1)}, u32[]{:S(2)}, u32[]{:S(2)}) async-start(bf16[8,144,512]{2,1,0:T(8,128)(2,1)} %bitcast.2), calls=%async_computation.1 | async-start | bytes 2359296 | tf_op jit(solution)/shard_map/all_to_all | solution.py:211
  63.3 1.6 copy-start
  92.6 41.7 %all-to-all-start.2 = ((bf16[8,144,512]{2,1,0:T(8,128)(2,1)}), bf16[8,144,512]{2,1,0:T(8,128)(2,1)S(1)}, u32[]{:S(2)}, u32[]{:S(2)}) async-start(bf16[8,144,512]{2,1,0:T(8,128)(2,1)} %bitcast.9), calls=%async_computation.2 | async-start | bytes 2359296 | tf_op jit(solution)/shard_map/all_to_all | solution.py:211
  96.2 107.9 %reduce-scatter.2.cloned.1.call-start = ((), (), s32[]{:S(2)}) async-start(), calls=%async_computation.6 | async-start | bytes 2359296 | tf_op jit(solution)/shard_map/reduce_scatter | solution.py:257
  96.4 1.6 copy-start.1
  134.3 1.6 copy-start.3
  154.7 47.1 %all-to-all-start.3 = ((bf16[8,144,512]{2,1,0:T(8,128)(2,1)}), bf16[8,144,512]{2,1,0:T(8,128)(2,1)S(1)}, u32[]{:S(2)}, u32[]{:S(2)}) async-start(bf16[8,144,512]{2,1,0:T(8,128)(2,1)} %bitcast.11), calls=%async_computation.3 | async-start | bytes 2359296 | tf_op jit(solution)/shard_map/all_to_all | solution.py:211
  161.4 21.5 %collective-permute-start = (bf16[192,2048]{1,0:T(8,128)(2,1)}, bf16[192,2048]{1,0:T(8,128)(2,1)S(1)}, u32[]{:S(2)}, u32[]{:S(2)}) collective-permute-start(bf16[192,2048]{1,0:T(8,128)(2,1)} %get-tuple-element.17), channel_id=1, source_target_pairs={{0,1},{1,2},{2,3},{3,0},{4,5},{5,6},{6,7},{7,4},{8,9},{9,10},{10,1... | collective-permute-start | bytes 2359304 | tf_op jit(solution)/shard_map/ppermute | solution.py:254
  162.9 36.4 %collective-permute-start.2 = (bf16[192,2048]{1,0:T(8,128)(2,1)}, bf16[192,2048]{1,0:T(8,128)(2,1)S(1)}, u32[]{:S(2)}, u32[]{:S(2)}) collective-permute-start(bf16[192,2048]{1,0:T(8,128)(2,1)} %get-tuple-element.18), channel_id=1, source_target_pairs={{0,3},{1,0},{2,1},{3,2},{4,7},{5,4},{6,5},{7,6},{8,11},{9,8},{10,9... | collective-permute-start | bytes 2359304 | tf_op jit(solution)/shard_map/ppermute | solution.py:254
  164.3 34.9 %collective-permute-start.1 = (bf16[192,2048]{1,0:T(8,128)(2,1)}, bf16[192,2048]{1,0:T(8,128)(2,1)S(1)}, u32[]{:S(2)}, u32[]{:S(2)}) collective-permute-start(bf16[192,2048]{1,0:T(8,128)(2,1)} %get-tuple-element.19), channel_id=1, source_target_pairs={{0,2},{1,3},{2,0},{3,1},{4,6},{5,7},{6,4},{7,5},{8,10},{9,11},{10,... | collective-permute-start | bytes 2359304 | tf_op jit(solution)/shard_map/ppermute | solution.py:254
Sparse Core Ops, SparseCore 0:
  9.8 46.6 all-gather.1
  106.1 41.2 reduce-scatter.1

commit v4 on v3

--- a/solution.py
+++ b/solution.py
@@ -234,6 +234,7 @@
         out_proj,
         full_grad,
     )
+    weight_part, got_grads = lax.optimization_barrier((weight_part, got_grads))
     back_grads_part, grad_k, grad_v = attend(
         backward_kernel,
         first,
@@ -243,16 +244,17 @@
         [slots, keys, keys],
         32,
     )
-    back_grads = exchange(back_grads_part)
     head_count = lax.axis_size("head")
     my_head = lax.axis_index("head")
     pieces = mixed_part.reshape(head_count, -1, width)
-    total = lax.dynamic_index_in_dim(pieces, my_head, 0, False).astype(jnp.float32)
+    arrived = [lax.dynamic_index_in_dim(pieces, my_head, 0, False)]
     for step in range(1, head_count):
         piece = lax.dynamic_index_in_dim(pieces, (my_head + step) % head_count, 0, False)
         pairs = [(i, (i + step) % head_count) for i in range(head_count)]
-        total = total + lax.ppermute(piece, "head", pairs).astype(jnp.float32)
-    mixed_out = total.astype(jnp.bfloat16)
+        arrived.append(lax.ppermute(piece, "head", pairs))
+    back_grads_part, arrived = lax.optimization_barrier((back_grads_part, arrived))
+    mixed_out = sum(x.astype(jnp.float32) for x in arrived).astype(jnp.bfloat16)
+    back_grads = exchange(back_grads_part)
     (grad_q,) = call(collect_kernel, [rows], move, local_docs, back_grads)
     grad_wo = lax.psum_scatter(weight_part, "seq", scatter_dimension=1, tiled=True).astype(
         jnp.float32

time: 214 us -> 213 us (level)
    all_to_all x4, waiting for transfers between devices: 79.3 us -> 97.2 us  [exchange(): return lax.all_to_all(x, 'seq', split_axis=0, concat_axis=0, tiled=True)]
    ppermute x3, waiting for transfers between devices: 33.4 us -> 15.8 us  [shards(): arrived.append(lax.ppermute(piece, 'head', pairs))]
    unnamed x12 -> x20, local copies, waits for them, and re-layouts: 5.91 us -> 7.08 us
where the time goes in v4:
time: 213 us; the launch traced here: 212 us
  waiting for transfers between devices  114 us (54%)
  Pallas kernels  47.8 us (22%)
  starting transfers between devices  21 us (10%)
  between operations  14.2 us (7%)
  local copies, waits for them, and re-layouts  10.3 us (5%)
  other arithmetic  4.9 us (2%)
    all_to_all x4, waiting for transfers between devices, exchange(): return lax.all_to_all(x, 'seq', split_axis=0, concat_axis=0, tiled=True)  97.2 us
    pallas_call x2, Pallas kernels, attend(): pl.pallas_call(kernel, grid_spec=pltpu.PrefetchScalarGridSpec(num_scalar_...  30.6 us
    all_to_all x4, starting transfers between devices, exchange(): return lax.all_to_all(x, 'seq', split_axis=0, concat_axis=0, tiled=True)  17.3 us
    pallas_call x4, Pallas kernels, call(): pl.pallas_call(kernel, out_shape=outs, in_specs=[whole] * len(operands),...  17.2 us
    ppermute x3, waiting for transfers between devices, shards(): arrived.append(lax.ppermute(piece, 'head', pairs))  15.8 us
    unnamed x20, local copies, waits for them, and re-layouts  7.08 us
  transfers between devices with their start and end apart: 9, of which 5 were waited for; matrix products, arithmetic and copies ran while one was open for 3% of the time, Pallas kernels for 23%

profile of v4, /device:TPU:0, one launch (start us, length us, event | category | flops | bytes accessed | tf_op | source)
XLA Modules:
  0.0 211.8 jit_solution(15802413704197772920)
XLA Ops:
  7.2 0.0 all-gather.2.cloned.1.call-start
  7.2 0.7 all-gather.2.cloned.1.call-update
  7.9 0.7 reshape.26
  8.7 0.0 copy-start.5
  8.7 1.1 copy-done.5
  9.8 2.3 %shard_map.110 = bf16[1152,512]{1,0:T(8,128)(2,1)} custom-call(s32[1,768]{1,0:T(1,128)S(1)} %constant_dynamic-slice_fusion.docs_ref, bf16[768,512]{1,0:T(8,128)(2,1)S(1)} %copy-done.5), custom_call_target="tpu_custom_call" | custom-call | flops 905969664 | bytes 1969152 | tf_op jit(solution)/shard_map/pallas_call | solution.py:159
  12.1 0.0 copy-start.9
  12.1 0.0 copy-start.3
  12.1 6.5 %all-to-all-start = ((bf16[8,144,512]{2,1,0:T(8,128)(2,1)}), bf16[8,144,512]{2,1,0:T(8,128)(2,1)S(1)}, u32[]{:S(2)}, u32[]{:S(2)}) async-start(bf16[8,144,512]{2,1,0:T(8,128)(2,1)} %bitcast), calls=%async_computation | async-start | bytes 2359296 | tf_op jit(solution)/shard_map/all_to_all | solution.py:211
  18.5 0.0 copy-done.9
  18.5 0.1 dynamic_slice.19
  18.6 0.1 select_reduce_fusion
  18.7 0.2 convert_reduce_fusion
  18.9 29.0 %all-to-all-done = bf16[8,144,512]{2,1,0:T(8,128)(2,1)S(1)} async-done(((bf16[8,144,512]{2,1,0:T(8,128)(2,1)}), bf16[8,144,512]{2,1,0:T(8,128)(2,1)S(1)}, u32[]{:S(2)}, u32[]{:S(2)}) %all-to-all-start) | async-done | bytes 1179680 | tf_op jit(solution)/shard_map/all_to_all | solution.py:211
  47.9 0.0 copy-done.3
  47.9 11.8 %shard_map.111 = bf16[1152,512]{1,0:T(8,128)(2,1)} custom-call(s32[8]{0:T(128)S(1)} %get-tuple-element.30.first_ref, s32[8]{0:T(128)S(1)} %get-tuple-element.29.count_ref, bf16[1152,512]{1,0:T(8,128)(2,1)S(1)} %bitcast.17, bf16[2048,512]{1,0:T(8,128)(2,1)S(1)} %copy-done.3, bf16[2048,512]{1,0:T(8,128)(2,1)} %v_ref.3), custom_call_target="tpu_custom_call" | custom-call | flops 2415919104 | bytes 16777216 | tf_op jit(solution)/shard_map/pallas_call | solution.py:174
  59.7 3.6 %all-to-all-start.1 = ((bf16[8,144,512]{2,1,0:T(8,128)(2,1)}), bf16[8,144,512]{2,1,0:T(8,128)(2,1)S(1)}, u32[]{:S(2)}, u32[]{:S(2)}) async-start(bf16[8,144,512]{2,1,0:T(8,128)(2,1)} %bitcast.2), calls=%async_computation.1 | async-start | bytes 2359296 | tf_op jit(solution)/shard_map/all_to_all | solution.py:211
  63.3 0.0 all-gather.2.cloned.1.call-done.grad_ref
  63.3 0.0 copy-start.1
  63.3 1.6 copy-done.1
  64.9 4.7 %shard_map.113 = bf16[1152,512]{1,0:T(8,128)(2,1)S(1)} custom-call(s32[1,768]{1,0:T(1,128)S(1)} %constant_dynamic-slice_fusion.docs_ref, bf16[768,2048]{1,0:T(8,128)(2,1)} %all-gather.2.cloned.1.call-done.grad_ref, bf16[512,2048]{1,0:T(8,128)(2,1)S(1)} %copy-done.1), custom_call_target="tpu_custom_call" | custom-call | flops 2516582400 | bytes 6425600 | tf_op jit(solution)/shard_map/pallas_call | solution.py:159
  69.6 0.0 copy-start
  69.7 1.0 copy-done
  70.7 22.0 %all-to-all-done.1 = bf16[8,144,512]{2,1,0:T(8,128)(2,1)S(1)} async-done(((bf16[8,144,512]{2,1,0:T(8,128)(2,1)}), bf16[8,144,512]{2,1,0:T(8,128)(2,1)S(1)}, u32[]{:S(2)}, u32[]{:S(2)}) %all-to-all-start.1) | async-done | bytes 1179680 | tf_op jit(solution)/shard_map/all_to_all | solution.py:211
  92.6 3.6 %all-to-all-start.2 = ((bf16[8,144,512]{2,1,0:T(8,128)(2,1)}), bf16[8,144,512]{2,1,0:T(8,128)(2,1)S(1)}, u32[]{:S(2)}, u32[]{:S(2)}) async-start(bf16[8,144,512]{2,1,0:T(8,128)(2,1)} %bitcast.21), calls=%async_computation.2 | async-start | bytes 2359296 | tf_op jit(solution)/shard_map/all_to_all | solution.py:211
  96.2 0.0 reduce-scatter.2.cloned.1.call-start
  96.3 0.0 copy-start.2
  96.3 1.6 copy-done.2
  97.8 7.9 %shard_map.112 = (bf16[768,2048]{1,0:T(8,128)(2,1)}, bf16[512,2048]{1,0:T(8,128)(2,1)}) custom-call(s32[1,768]{1,0:T(1,128)S(1)} %constant_dynamic-slice_fusion.docs_ref, bf16[1152,512]{1,0:T(8,128)(2,1)S(1)} %bitcast.20, bf16[512,2048]{1,0:T(8,128)(2,1)S(1)} %copy-done.2, bf16[768,2048]{1,0:T(8,128)(2,1)} %all-gather.2.cloned.1.call-done.grad_ref), custom_call_target="tpu_custom_call" | custom-call | flops 4127195136 | bytes 11668480 | tf_op jit(solution)/shard_map/pallas_call | solution.py:159
  105.8 19.7 %all-to-all-done.2 = bf16[8,144,512]{2,1,0:T(8,128)(2,1)S(1)} async-done(((bf16[8,144,512]{2,1,0:T(8,128)(2,1)}), bf16[8,144,512]{2,1,0:T(8,128)(2,1)S(1)}, u32[]{:S(2)}, u32[]{:S(2)}) %all-to-all-start.2) | async-done | bytes 1179680 | tf_op jit(solution)/shard_map/all_to_all | solution.py:211
  125.5 0.0 reduce-scatter.2.cloned.1.call-update
  125.6 0.0 copy-start.4
  125.6 2.4 %dynamic-slice_bitcast_fusion = (bf16[192,2048]{1,0:T(8,128)(2,1)S(1)}, bf16[192,2048]{1,0:T(8,128)(2,1)S(1)}, bf16[192,2048]{1,0:T(8,128)(2,1)S(1)}, bf16[192,2048]{1,0:T(8,128)(2,1)S(1)}) fusion(bf16[4,192,2048]{2,1,0:T(8,128)(2,1)} %bitcast.23, s32[]{:T(128)S(6)} %select_n.53, s32[]{:T(128)S(6)} %select_n.51, s32[]{:T(128)S(6)} %select_n.49, s32[]{:T(128)S(6)} %select_n.47), kind=kLoop, calls=%fused_computation.1 | loop fusion | bytes 6291472 | tf_op jit(solution)/shard_map/jit(dynamic_index_in_dim)/squeeze | solution.py:252
  128.0 2.5 %collective-permute-start.2 = (bf16[192,2048]{1,0:T(8,128)(2,1)S(1)}, bf16[192,2048]{1,0:T(8,128)(2,1)}, u32[]{:S(2)}, u32[]{:S(2)}) collective-permute-start(bf16[192,2048]{1,0:T(8,128)(2,1)S(1)} %get-tuple-element.31), channel_id=1, source_target_pairs={{0,3},{1,0},{2,1},{3,2},{4,7},{5,4},{6,5},{7,6},{8,11},{9,8},{10,9... | collective-permute-start | bytes 2359304 | tf_op jit(solution)/shard_map/ppermute | solution.py:254
  130.5 0.5 collective-permute-start.1
  131.0 0.6 collective-permute-start
  131.6 0.0 copy-done.4
  131.6 18.8 %shard_map.114 = (bf16[1152,512]{1,0:T(8,128)(2,1)}, bf16[2048,512]{1,0:T(8,128)(2,1)}, bf16[2048,512]{1,0:T(8,128)(2,1)}) custom-call(s32[8]{0:T(128)S(1)} %get-tuple-element.30.first_ref, s32[8]{0:T(128)S(1)} %get-tuple-element.29.count_ref, bf16[1152,512]{1,0:T(8,128)(2,1)S(1)} %bitcast.18, bf16[1152,512]{1,0:T(8,128)(2,1)S(1)} %bitcast.19, ...), custom_call_target="tpu_custom_call" | custom-call | flops 4831838208 | bytes 16777216 | tf_op jit(solution)/shard_map/pallas_call | solution.py:174
  150.4 0.0 collective-permute-done.2
  150.4 15.8 %collective-permute-done.1 = bf16[192,2048]{1,0:T(8,128)(2,1)S(1)} collective-permute-done((bf16[192,2048]{1,0:T(8,128)(2,1)S(1)}, bf16[192,2048]{1,0:T(8,128)(2,1)S(1)}, u32[]{:S(2)}, u32[]{:S(2)}) %collective-permute-start.1) | collective-permute-done | bytes 786464 | tf_op jit(solution)/shard_map/ppermute | solution.py:254
  166.1 0.0 copy-start.6
  166.1 0.0 collective-permute-done
  166.1 0.9 copy-done.6
  167.0 0.0 copy-start.8
  167.0 0.9 copy-done.8
  167.9 0.0 copy-start.7
  167.9 3.7 %all-to-all-start.3 = ((bf16[8,144,512]{2,1,0:T(8,128)(2,1)}), bf16[8,144,512]{2,1,0:T(8,128)(2,1)S(1)}, u32[]{:S(2)}, u32[]{:S(2)}) async-start(bf16[8,144,512]{2,1,0:T(8,128)(2,1)} %bitcast.11), calls=%async_computation.3 | async-start | bytes 2359296 | tf_op jit(solution)/shard_map/all_to_all | solution.py:211
  171.6 0.0 copy-done.7
  171.6 2.8 %add_convert_fusion = bf16[192,2048]{1,0:T(8,128)(2,1)} fusion(bf16[192,2048]{1,0:T(8,128)(2,1)} %collective-permute-done.2, bf16[192,2048]{1,0:T(8,128)(2,1)S(1)} %copy-done.7, bf16[192,2048]{1,0:T(8,128)(2,1)} %copy-done.8, bf16[192,2048]{1,0:T(8,128)(2,1)S(1)} %get-tuple-element.21), kind=kLoop, calls=%fused_computation | loop fusion | flops 3145728 | bytes 3932160 | tf_op jit(solution)/shard_map/convert_element_type | solution.py:256
  174.4 26.5 %all-to-all-done.3 = bf16[8,144,512]{2,1,0:T(8,128)(2,1)S(1)} async-done(((bf16[8,144,512]{2,1,0:T(8,128)(2,1)}), bf16[8,144,512]{2,1,0:T(8,128)(2,1)S(1)}, u32[]{:S(2)}, u32[]{:S(2)}) %all-to-all-start.3) | async-done | bytes 1179680 | tf_op jit(solution)/shard_map/all_to_all | solution.py:211
  200.9 2.3 %shard_map.115 = bf16[768,512]{1,0:T(8,128)(2,1)} custom-call(s32[1,768]{1,0:T(1,128)S(1)} %constant_dynamic-slice_fusion.docs_ref, bf16[1152,512]{1,0:T(8,128)(2,1)S(1)} %bitcast.22), custom_call_target="tpu_custom_call" | custom-call | flops 905969664 | bytes 1969152 | tf_op jit(solution)/shard_map/pallas_call | solution.py:159
  203.2 0.0 reduce-scatter.2.cloned.1.call-done
  203.2 1.8 convert_element_type.31
  (1 shorter events, 0.0 us)
Async XLA Ops:
  7.2 56.2 %all-gather.2.cloned.1.call-start = ((), (), s32[]{:S(2)}) async-start(), calls=%async_computation.5 | async-start | bytes 3932160 | tf_op jit(solution)/shard_map/all_gather | solution.py:213
  8.7 1.1 copy-start.5
  12.1 6.5 %copy-start.9 = (s32[128]{0:T(128)S(1)}, s32[128]{0:T(128)}, u32[]{:S(2)}) copy-start(s32[128]{0:T(128)} %param.12) | copy-start | bytes 1540
  12.1 35.9 %copy-start.3 = (bf16[2048,512]{1,0:T(8,128)(2,1)S(1)}, bf16[2048,512]{1,0:T(8,128)(2,1)}, u32[]{:S(2)}) copy-start(bf16[2048,512]{1,0:T(8,128)(2,1)} %k_ref.3) | copy-start | bytes 6291460
  12.1 35.9 %all-to-all-start = ((bf16[8,144,512]{2,1,0:T(8,128)(2,1)}), bf16[8,144,512]{2,1,0:T(8,128)(2,1)S(1)}, u32[]{:S(2)}, u32[]{:S(2)}) async-start(bf16[8,144,512]{2,1,0:T(8,128)(2,1)} %bitcast), calls=%async_computation | async-start | bytes 2359296 | tf_op jit(solution)/shard_map/all_to_all | solution.py:211
  59.7 32.9 %all-to-all-start.1 = ((bf16[8,144,512]{2,1,0:T(8,128)(2,1)}), bf16[8,144,512]{2,1,0:T(8,128)(2,1)S(1)}, u32[]{:S(2)}, u32[]{:S(2)}) async-start(bf16[8,144,512]{2,1,0:T(8,128)(2,1)} %bitcast.2), calls=%async_computation.1 | async-start | bytes 2359296 | tf_op jit(solution)/shard_map/all_to_all | solution.py:211
  63.3 1.6 copy-start.1
  69.6 1.0 copy-start
  92.6 32.9 %all-to-all-start.2 = ((bf16[8,144,512]{2,1,0:T(8,128)(2,1)}), bf16[8,144,512]{2,1,0:T(8,128)(2,1)S(1)}, u32[]{:S(2)}, u32[]{:S(2)}) async-start(bf16[8,144,512]{2,1,0:T(8,128)(2,1)} %bitcast.21), calls=%async_computation.2 | async-start | bytes 2359296 | tf_op jit(solution)/shard_map/all_to_all | solution.py:211
  96.2 107.0 %reduce-scatter.2.cloned.1.call-start = ((), (), s32[]{:S(2)}) async-start(), calls=%async_computation.6 | async-start | bytes 2359296 | tf_op jit(solution)/shard_map/reduce_scatter | solution.py:259
  96.3 1.6 copy-start.2
  125.6 6.0 %copy-start.4 = (bf16[2048,512]{1,0:T(8,128)(2,1)S(1)}, bf16[2048,512]{1,0:T(8,128)(2,1)}, u32[]{:S(2)}) copy-start(bf16[2048,512]{1,0:T(8,128)(2,1)} %k_ref.3) | copy-start | bytes 6291460
  128.0 22.4 %collective-permute-start.2 = (bf16[192,2048]{1,0:T(8,128)(2,1)S(1)}, bf16[192,2048]{1,0:T(8,128)(2,1)}, u32[]{:S(2)}, u32[]{:S(2)}) collective-permute-start(bf16[192,2048]{1,0:T(8,128)(2,1)S(1)} %get-tuple-element.31), channel_id=1, source_target_pairs={{0,3},{1,0},{2,1},{3,2},{4,7},{5,4},{6,5},{7,6},{8,11},{9,8},{10,9... | collective-permute-start | bytes 2359304 | tf_op jit(solution)/shard_map/ppermute | solution.py:254
  130.5 35.7 %collective-permute-start.1 = (bf16[192,2048]{1,0:T(8,128)(2,1)S(1)}, bf16[192,2048]{1,0:T(8,128)(2,1)S(1)}, u32[]{:S(2)}, u32[]{:S(2)}) collective-permute-start(bf16[192,2048]{1,0:T(8,128)(2,1)S(1)} %get-tuple-element.32), channel_id=1, source_target_pairs={{0,2},{1,3},{2,0},{3,1},{4,6},{5,7},{6,4},{7,5},{8,10},{9,11},{10,... | collective-permute-start | bytes 2359304 | tf_op jit(solution)/shard_map/ppermute | solution.py:254
  131.0 35.2 %collective-permute-start = (bf16[192,2048]{1,0:T(8,128)(2,1)S(1)}, bf16[192,2048]{1,0:T(8,128)(2,1)S(1)}, u32[]{:S(2)}, u32[]{:S(2)}) collective-permute-start(bf16[192,2048]{1,0:T(8,128)(2,1)S(1)} %get-tuple-element.33), channel_id=1, source_target_pairs={{0,1},{1,2},{2,3},{3,0},{4,5},{5,6},{6,7},{7,4},{8,9},{9,10},{10,1... | collective-permute-start | bytes 2359304 | tf_op jit(solution)/shard_map/ppermute | solution.py:254
  166.1 0.9 copy-start.6
  167.0 0.9 copy-start.8
  167.9 3.7 %copy-start.7 = (bf16[192,2048]{1,0:T(8,128)(2,1)S(1)}, bf16[192,2048]{1,0:T(8,128)(2,1)}, u32[]{:S(2)}) copy-start(bf16[192,2048]{1,0:T(8,128)(2,1)} %copy-done.6) | copy-start | bytes 2359300
  167.9 33.0 %all-to-all-start.3 = ((bf16[8,144,512]{2,1,0:T(8,128)(2,1)}), bf16[8,144,512]{2,1,0:T(8,128)(2,1)S(1)}, u32[]{:S(2)}, u32[]{:S(2)}) async-start(bf16[8,144,512]{2,1,0:T(8,128)(2,1)} %bitcast.11), calls=%async_computation.3 | async-start | bytes 2359296 | tf_op jit(solution)/shard_map/all_to_all | solution.py:211
Sparse Core Ops, SparseCore 0:
  9.8 46.6 all-gather.1
  125.7 34.5 reduce-scatter.1
